TPU v7x, 256 devices: a whole 4x4x8 slice. The times are simulated.
256 devices in a mesh: tm: 64 (over x, y_lo, z), gz: 4 (over y_hi, core).
Axes of the slice: x: 4, y: 4 (y_hi: 2, y_lo: 2; y = y_hi * 2 + y_lo), z: 8, core: 2. Of those that a mesh axis runs over, the one named last changes fastest.
Arguments:
- states: float32 [64, 3, 64, 16, 128], P('tm', None, 'gz'), may hold values from -4 to 4
- rate: float32 [64, 16, 128], P('gz'), may hold values from 0.1 to 40
Outputs:
- new_states: float32 [64, 3, 64, 16, 128], P('tm', None, 'gz')
All inputs are finite; a program needn't handle non-finite values.
Results may differ from a plain program's by a relative error of at most 0.000044.
Values sent between devices are 32-bit elements; how exact they have to be, the bound alone decides.
A program may use at most 128 MiB of HBM per device.

v0:
```python
import jax
import jax.numpy as jnp
from jax import lax
from jax.sharding import PartitionSpec as P

STEPS = 2


VISCOSITY = 0.05
TIME_STEP = 0.2


def padded_2(cells, sides, width):
    for axis, dim in sides:
        count = lax.axis_size(axis)
        head = lax.slice_in_dim(cells, 0, width, axis=dim)
        tail = lax.slice_in_dim(cells, cells.shape[dim] - width, cells.shape[dim], axis=dim)
        cells = jnp.concatenate(
            [
                lax.ppermute(tail, axis, [(i, (i + 1) % count) for i in range(count)]),
                cells,
                lax.ppermute(head, axis, [((i + 1) % count, i) for i in range(count)]),
            ],
            axis=dim,
        )
    return cells


def passed_along(value, axis, steps):
    count = lax.axis_size(axis)
    first, last = (max(0, -steps), min(count, count - steps))
    return lax.ppermute(value, axis, [(source, source + steps) for source in range(first, last)])


def tendency(padded):
    core = padded[:, 1:-1]
    along_x = (jnp.roll(core, -1, 3) - jnp.roll(core, 1, 3)) * 0.5
    along_y = (jnp.roll(core, -1, 2) - jnp.roll(core, 1, 2)) * 0.5
    along_z = (padded[:, 2:] - padded[:, :-2]) * 0.5
    spread = (
        jnp.roll(core, -1, 3) + jnp.roll(core, 1, 3) + jnp.roll(core, -1, 2) + jnp.roll(core, 1, 2)
    )
    spread = spread + padded[:, 2:] + padded[:, :-2] - 6.0 * core
    advect = core[0:1] * along_x + core[1:2] * along_y + core[2:3] * along_z
    return -advect + VISCOSITY * spread


def shallow_rate(field):
    return tendency(padded_2(field, (("gz", 1),), 1))


def fine_shallow(field):
    for step in range(STEPS):
        first = field + TIME_STEP * shallow_rate(field)
        second = 0.75 * field + 0.25 * (first + TIME_STEP * shallow_rate(first))
        field = 1.0 / 3.0 * field + 2.0 / 3.0 * (second + TIME_STEP * shallow_rate(second))
    return field


def shards(states, rate):
    slices = lax.axis_size("tm")
    damp = jnp.exp(-rate / slices)
    own = states[0]
    finished = fine_shallow(own)
    jump = finished - damp * own
    leading = lax.axis_index("tm") == 0

    def relay_turn(turn, current):
        outgoing = damp * current + jump
        incoming = passed_along(outgoing, "tm", 1)
        return jnp.where(leading, own, incoming)

    updated = lax.fori_loop(0, slices - 1, relay_turn, own)
    return updated[None]


def solution(mesh):
    return jax.shard_map(
        shards,
        mesh=mesh,
        in_specs=(P("tm", None, "gz", None, None), P("gz", None, None)),
        out_specs=P("tm", None, "gz", None, None),
        check_vma=False,
    )
```

profile of v0, /device:TPU:6, one launch (start us, length us, event | category | flops | bytes accessed | tf_op | source)
XLA Modules:
  0.0 943.2 jit_solution(6391867870855737078)
XLA Ops:
  45.3 897.1 %while.10 = (s32[]{:T(128)}, f32[3,16,16,128]{3,2,1,0:T(8,128)S(1)}, pred[]{:T(512)}, f32[16,16,128]{2,1,0:T(8,128)S(1)}, f32[3,16,16,128]{3,2,1,0:T(8,128)S(1)}, /*index=5*/f32[3,16,16,128]{3,2,1,0:T(8,128)S(1)}, s32[]{:T(128)}) while((s32[]{:T(128)}, f32[3,16,16,128]{3,2,1,0:T(8,128)S(1)}, pred[]{:T(512)}, f32[16,16,128]{2,1,0:T(8,128)S(1)}, ...), condition=%wide.region_1.2_spmd, body=%wide.region_0.1_spmd.sunk | while | flops 294914 | bytes 4063350 | solution.py:73
  49.2 11.1 %collective-permute-done = f32[3,16,16,128]{3,2,1,0:T(8,128)S(1)} collective-permute-done((f32[3,16,16,128]{3,2,1,0:T(8,128)S(1)}, f32[3,16,16,128]{3,2,1,0:T(8,128)S(1)}, u32[]{:S(2)}, u32[]{:S(2)}) %collective-permute-start) | collective-permute-done | bytes 393248 | tf_op jit(solution)/shard_map/while/body/eval_jaxpr/ppermute | solution.py:32
  62.4 11.5 %collective-permute-done = f32[3,16,16,128]{3,2,1,0:T(8,128)S(1)} collective-permute-done((f32[3,16,16,128]{3,2,1,0:T(8,128)S(1)}, f32[3,16,16,128]{3,2,1,0:T(8,128)S(1)}, u32[]{:S(2)}, u32[]{:S(2)}) %collective-permute-start) | collective-permute-done | bytes 393248 | tf_op jit(solution)/shard_map/while/body/eval_jaxpr/ppermute | solution.py:32
  88.7 10.8 %collective-permute-done = f32[3,16,16,128]{3,2,1,0:T(8,128)S(1)} collective-permute-done((f32[3,16,16,128]{3,2,1,0:T(8,128)S(1)}, f32[3,16,16,128]{3,2,1,0:T(8,128)S(1)}, u32[]{:S(2)}, u32[]{:S(2)}) %collective-permute-start) | collective-permute-done | bytes 393248 | tf_op jit(solution)/shard_map/while/body/eval_jaxpr/ppermute | solution.py:32
  114.3 11.1 %collective-permute-done = f32[3,16,16,128]{3,2,1,0:T(8,128)S(1)} collective-permute-done((f32[3,16,16,128]{3,2,1,0:T(8,128)S(1)}, f32[3,16,16,128]{3,2,1,0:T(8,128)S(1)}, u32[]{:S(2)}, u32[]{:S(2)}) %collective-permute-start) | collective-permute-done | bytes 393248 | tf_op jit(solution)/shard_map/while/body/eval_jaxpr/ppermute | solution.py:32
  127.5 12.2 %collective-permute-done = f32[3,16,16,128]{3,2,1,0:T(8,128)S(1)} collective-permute-done((f32[3,16,16,128]{3,2,1,0:T(8,128)S(1)}, f32[3,16,16,128]{3,2,1,0:T(8,128)S(1)}, u32[]{:S(2)}, u32[]{:S(2)}) %collective-permute-start) | collective-permute-done | bytes 393248 | tf_op jit(solution)/shard_map/while/body/eval_jaxpr/ppermute | solution.py:32
  141.8 13.3 %collective-permute-done = f32[3,16,16,128]{3,2,1,0:T(8,128)S(1)} collective-permute-done((f32[3,16,16,128]{3,2,1,0:T(8,128)S(1)}, f32[3,16,16,128]{3,2,1,0:T(8,128)S(1)}, u32[]{:S(2)}, u32[]{:S(2)}) %collective-permute-start) | collective-permute-done | bytes 393248 | tf_op jit(solution)/shard_map/while/body/eval_jaxpr/ppermute | solution.py:32
  157.1 14.5 %collective-permute-done = f32[3,16,16,128]{3,2,1,0:T(8,128)S(1)} collective-permute-done((f32[3,16,16,128]{3,2,1,0:T(8,128)S(1)}, f32[3,16,16,128]{3,2,1,0:T(8,128)S(1)}, u32[]{:S(2)}, u32[]{:S(2)}) %collective-permute-start) | collective-permute-done | bytes 393248 | tf_op jit(solution)/shard_map/while/body/eval_jaxpr/ppermute | solution.py:32
  173.7 14.3 %collective-permute-done = f32[3,16,16,128]{3,2,1,0:T(8,128)S(1)} collective-permute-done((f32[3,16,16,128]{3,2,1,0:T(8,128)S(1)}, f32[3,16,16,128]{3,2,1,0:T(8,128)S(1)}, u32[]{:S(2)}, u32[]{:S(2)}) %collective-permute-start) | collective-permute-done | bytes 393248 | tf_op jit(solution)/shard_map/while/body/eval_jaxpr/ppermute | solution.py:32
  190.0 13.5 %collective-permute-done = f32[3,16,16,128]{3,2,1,0:T(8,128)S(1)} collective-permute-done((f32[3,16,16,128]{3,2,1,0:T(8,128)S(1)}, f32[3,16,16,128]{3,2,1,0:T(8,128)S(1)}, u32[]{:S(2)}, u32[]{:S(2)}) %collective-permute-start) | collective-permute-done | bytes 393248 | tf_op jit(solution)/shard_map/while/body/eval_jaxpr/ppermute | solution.py:32
  205.6 12.6 %collective-permute-done = f32[3,16,16,128]{3,2,1,0:T(8,128)S(1)} collective-permute-done((f32[3,16,16,128]{3,2,1,0:T(8,128)S(1)}, f32[3,16,16,128]{3,2,1,0:T(8,128)S(1)}, u32[]{:S(2)}, u32[]{:S(2)}) %collective-permute-start) | collective-permute-done | bytes 393248 | tf_op jit(solution)/shard_map/while/body/eval_jaxpr/ppermute | solution.py:32
  220.2 11.6 %collective-permute-done = f32[3,16,16,128]{3,2,1,0:T(8,128)S(1)} collective-permute-done((f32[3,16,16,128]{3,2,1,0:T(8,128)S(1)}, f32[3,16,16,128]{3,2,1,0:T(8,128)S(1)}, u32[]{:S(2)}, u32[]{:S(2)}) %collective-permute-start) | collective-permute-done | bytes 393248 | tf_op jit(solution)/shard_map/while/body/eval_jaxpr/ppermute | solution.py:32
  233.9 10.8 %collective-permute-done = f32[3,16,16,128]{3,2,1,0:T(8,128)S(1)} collective-permute-done((f32[3,16,16,128]{3,2,1,0:T(8,128)S(1)}, f32[3,16,16,128]{3,2,1,0:T(8,128)S(1)}, u32[]{:S(2)}, u32[]{:S(2)}) %collective-permute-start) | collective-permute-done | bytes 393248 | tf_op jit(solution)/shard_map/while/body/eval_jaxpr/ppermute | solution.py:32
  259.5 10.8 %collective-permute-done = f32[3,16,16,128]{3,2,1,0:T(8,128)S(1)} collective-permute-done((f32[3,16,16,128]{3,2,1,0:T(8,128)S(1)}, f32[3,16,16,128]{3,2,1,0:T(8,128)S(1)}, u32[]{:S(2)}, u32[]{:S(2)}) %collective-permute-start) | collective-permute-done | bytes 393248 | tf_op jit(solution)/shard_map/while/body/eval_jaxpr/ppermute | solution.py:32
  272.3 10.9 %collective-permute-done = f32[3,16,16,128]{3,2,1,0:T(8,128)S(1)} collective-permute-done((f32[3,16,16,128]{3,2,1,0:T(8,128)S(1)}, f32[3,16,16,128]{3,2,1,0:T(8,128)S(1)}, u32[]{:S(2)}, u32[]{:S(2)}) %collective-permute-start) | collective-permute-done | bytes 393248 | tf_op jit(solution)/shard_map/while/body/eval_jaxpr/ppermute | solution.py:32
  285.3 12.0 %collective-permute-done = f32[3,16,16,128]{3,2,1,0:T(8,128)S(1)} collective-permute-done((f32[3,16,16,128]{3,2,1,0:T(8,128)S(1)}, f32[3,16,16,128]{3,2,1,0:T(8,128)S(1)}, u32[]{:S(2)}, u32[]{:S(2)}) %collective-permute-start) | collective-permute-done | bytes 393248 | tf_op jit(solution)/shard_map/while/body/eval_jaxpr/ppermute | solution.py:32
  299.4 13.1 %collective-permute-done = f32[3,16,16,128]{3,2,1,0:T(8,128)S(1)} collective-permute-done((f32[3,16,16,128]{3,2,1,0:T(8,128)S(1)}, f32[3,16,16,128]{3,2,1,0:T(8,128)S(1)}, u32[]{:S(2)}, u32[]{:S(2)}) %collective-permute-start) | collective-permute-done | bytes 393248 | tf_op jit(solution)/shard_map/while/body/eval_jaxpr/ppermute | solution.py:32
  314.5 14.3 %collective-permute-done = f32[3,16,16,128]{3,2,1,0:T(8,128)S(1)} collective-permute-done((f32[3,16,16,128]{3,2,1,0:T(8,128)S(1)}, f32[3,16,16,128]{3,2,1,0:T(8,128)S(1)}, u32[]{:S(2)}, u32[]{:S(2)}) %collective-permute-start) | collective-permute-done | bytes 393248 | tf_op jit(solution)/shard_map/while/body/eval_jaxpr/ppermute | solution.py:32
  330.9 14.5 %collective-permute-done = f32[3,16,16,128]{3,2,1,0:T(8,128)S(1)} collective-permute-done((f32[3,16,16,128]{3,2,1,0:T(8,128)S(1)}, f32[3,16,16,128]{3,2,1,0:T(8,128)S(1)}, u32[]{:S(2)}, u32[]{:S(2)}) %collective-permute-start) | collective-permute-done | bytes 393248 | tf_op jit(solution)/shard_map/while/body/eval_jaxpr/ppermute | solution.py:32
  347.4 13.7 %collective-permute-done = f32[3,16,16,128]{3,2,1,0:T(8,128)S(1)} collective-permute-done((f32[3,16,16,128]{3,2,1,0:T(8,128)S(1)}, f32[3,16,16,128]{3,2,1,0:T(8,128)S(1)}, u32[]{:S(2)}, u32[]{:S(2)}) %collective-permute-start) | collective-permute-done | bytes 393248 | tf_op jit(solution)/shard_map/while/body/eval_jaxpr/ppermute | solution.py:32
  363.2 12.8 %collective-permute-done = f32[3,16,16,128]{3,2,1,0:T(8,128)S(1)} collective-permute-done((f32[3,16,16,128]{3,2,1,0:T(8,128)S(1)}, f32[3,16,16,128]{3,2,1,0:T(8,128)S(1)}, u32[]{:S(2)}, u32[]{:S(2)}) %collective-permute-start) | collective-permute-done | bytes 393248 | tf_op jit(solution)/shard_map/while/body/eval_jaxpr/ppermute | solution.py:32
  378.1 11.9 %collective-permute-done = f32[3,16,16,128]{3,2,1,0:T(8,128)S(1)} collective-permute-done((f32[3,16,16,128]{3,2,1,0:T(8,128)S(1)}, f32[3,16,16,128]{3,2,1,0:T(8,128)S(1)}, u32[]{:S(2)}, u32[]{:S(2)}) %collective-permute-start) | collective-permute-done | bytes 393248 | tf_op jit(solution)/shard_map/while/body/eval_jaxpr/ppermute | solution.py:32
  392.1 11.0 %collective-permute-done = f32[3,16,16,128]{3,2,1,0:T(8,128)S(1)} collective-permute-done((f32[3,16,16,128]{3,2,1,0:T(8,128)S(1)}, f32[3,16,16,128]{3,2,1,0:T(8,128)S(1)}, u32[]{:S(2)}, u32[]{:S(2)}) %collective-permute-start) | collective-permute-done | bytes 393248 | tf_op jit(solution)/shard_map/while/body/eval_jaxpr/ppermute | solution.py:32
  443.6 11.6 %collective-permute-done = f32[3,16,16,128]{3,2,1,0:T(8,128)S(1)} collective-permute-done((f32[3,16,16,128]{3,2,1,0:T(8,128)S(1)}, f32[3,16,16,128]{3,2,1,0:T(8,128)S(1)}, u32[]{:S(2)}, u32[]{:S(2)}) %collective-permute-start) | collective-permute-done | bytes 393248 | tf_op jit(solution)/shard_map/while/body/eval_jaxpr/ppermute | solution.py:32
  457.2 12.7 %collective-permute-done = f32[3,16,16,128]{3,2,1,0:T(8,128)S(1)} collective-permute-done((f32[3,16,16,128]{3,2,1,0:T(8,128)S(1)}, f32[3,16,16,128]{3,2,1,0:T(8,128)S(1)}, u32[]{:S(2)}, u32[]{:S(2)}) %collective-permute-start) | collective-permute-done | bytes 393248 | tf_op jit(solution)/shard_map/while/body/eval_jaxpr/ppermute | solution.py:32
  472.0 13.8 %collective-permute-done = f32[3,16,16,128]{3,2,1,0:T(8,128)S(1)} collective-permute-done((f32[3,16,16,128]{3,2,1,0:T(8,128)S(1)}, f32[3,16,16,128]{3,2,1,0:T(8,128)S(1)}, u32[]{:S(2)}, u32[]{:S(2)}) %collective-permute-start) | collective-permute-done | bytes 393248 | tf_op jit(solution)/shard_map/while/body/eval_jaxpr/ppermute | solution.py:32
  487.8 14.9 %collective-permute-done = f32[3,16,16,128]{3,2,1,0:T(8,128)S(1)} collective-permute-done((f32[3,16,16,128]{3,2,1,0:T(8,128)S(1)}, f32[3,16,16,128]{3,2,1,0:T(8,128)S(1)}, u32[]{:S(2)}, u32[]{:S(2)}) %collective-permute-start) | collective-permute-done | bytes 393248 | tf_op jit(solution)/shard_map/while/body/eval_jaxpr/ppermute | solution.py:32
  504.8 14.1 %collective-permute-done = f32[3,16,16,128]{3,2,1,0:T(8,128)S(1)} collective-permute-done((f32[3,16,16,128]{3,2,1,0:T(8,128)S(1)}, f32[3,16,16,128]{3,2,1,0:T(8,128)S(1)}, u32[]{:S(2)}, u32[]{:S(2)}) %collective-permute-start) | collective-permute-done | bytes 393248 | tf_op jit(solution)/shard_map/while/body/eval_jaxpr/ppermute | solution.py:32
  521.0 13.3 %collective-permute-done = f32[3,16,16,128]{3,2,1,0:T(8,128)S(1)} collective-permute-done((f32[3,16,16,128]{3,2,1,0:T(8,128)S(1)}, f32[3,16,16,128]{3,2,1,0:T(8,128)S(1)}, u32[]{:S(2)}, u32[]{:S(2)}) %collective-permute-start) | collective-permute-done | bytes 393248 | tf_op jit(solution)/shard_map/while/body/eval_jaxpr/ppermute | solution.py:32
  536.3 12.4 %collective-permute-done = f32[3,16,16,128]{3,2,1,0:T(8,128)S(1)} collective-permute-done((f32[3,16,16,128]{3,2,1,0:T(8,128)S(1)}, f32[3,16,16,128]{3,2,1,0:T(8,128)S(1)}, u32[]{:S(2)}, u32[]{:S(2)}) %collective-permute-start) | collective-permute-done | bytes 393248 | tf_op jit(solution)/shard_map/while/body/eval_jaxpr/ppermute | solution.py:32
  550.7 11.4 %collective-permute-done = f32[3,16,16,128]{3,2,1,0:T(8,128)S(1)} collective-permute-done((f32[3,16,16,128]{3,2,1,0:T(8,128)S(1)}, f32[3,16,16,128]{3,2,1,0:T(8,128)S(1)}, u32[]{:S(2)}, u32[]{:S(2)}) %collective-permute-start) | collective-permute-done | bytes 393248 | tf_op jit(solution)/shard_map/while/body/eval_jaxpr/ppermute | solution.py:32
  577.0 10.8 %collective-permute-done = f32[3,16,16,128]{3,2,1,0:T(8,128)S(1)} collective-permute-done((f32[3,16,16,128]{3,2,1,0:T(8,128)S(1)}, f32[3,16,16,128]{3,2,1,0:T(8,128)S(1)}, u32[]{:S(2)}, u32[]{:S(2)}) %collective-permute-start) | collective-permute-done | bytes 393248 | tf_op jit(solution)/shard_map/while/body/eval_jaxpr/ppermute | solution.py:32
  602.7 11.1 %collective-permute-done = f32[3,16,16,128]{3,2,1,0:T(8,128)S(1)} collective-permute-done((f32[3,16,16,128]{3,2,1,0:T(8,128)S(1)}, f32[3,16,16,128]{3,2,1,0:T(8,128)S(1)}, u32[]{:S(2)}, u32[]{:S(2)}) %collective-permute-start) | collective-permute-done | bytes 393248 | tf_op jit(solution)/shard_map/while/body/eval_jaxpr/ppermute | solution.py:32
  615.9 12.2 %collective-permute-done = f32[3,16,16,128]{3,2,1,0:T(8,128)S(1)} collective-permute-done((f32[3,16,16,128]{3,2,1,0:T(8,128)S(1)}, f32[3,16,16,128]{3,2,1,0:T(8,128)S(1)}, u32[]{:S(2)}, u32[]{:S(2)}) %collective-permute-start) | collective-permute-done | bytes 393248 | tf_op jit(solution)/shard_map/while/body/eval_jaxpr/ppermute | solution.py:32
  630.1 13.3 %collective-permute-done = f32[3,16,16,128]{3,2,1,0:T(8,128)S(1)} collective-permute-done((f32[3,16,16,128]{3,2,1,0:T(8,128)S(1)}, f32[3,16,16,128]{3,2,1,0:T(8,128)S(1)}, u32[]{:S(2)}, u32[]{:S(2)}) %collective-permute-start) | collective-permute-done | bytes 393248 | tf_op jit(solution)/shard_map/while/body/eval_jaxpr/ppermute | solution.py:32
  645.5 14.5 %collective-permute-done = f32[3,16,16,128]{3,2,1,0:T(8,128)S(1)} collective-permute-done((f32[3,16,16,128]{3,2,1,0:T(8,128)S(1)}, f32[3,16,16,128]{3,2,1,0:T(8,128)S(1)}, u32[]{:S(2)}, u32[]{:S(2)}) %collective-permute-start) | collective-permute-done | bytes 393248 | tf_op jit(solution)/shard_map/while/body/eval_jaxpr/ppermute | solution.py:32
  662.1 14.3 %collective-permute-done = f32[3,16,16,128]{3,2,1,0:T(8,128)S(1)} collective-permute-done((f32[3,16,16,128]{3,2,1,0:T(8,128)S(1)}, f32[3,16,16,128]{3,2,1,0:T(8,128)S(1)}, u32[]{:S(2)}, u32[]{:S(2)}) %collective-permute-start) | collective-permute-done | bytes 393248 | tf_op jit(solution)/shard_map/while/body/eval_jaxpr/ppermute | solution.py:32
  678.4 13.5 %collective-permute-done = f32[3,16,16,128]{3,2,1,0:T(8,128)S(1)} collective-permute-done((f32[3,16,16,128]{3,2,1,0:T(8,128)S(1)}, f32[3,16,16,128]{3,2,1,0:T(8,128)S(1)}, u32[]{:S(2)}, u32[]{:S(2)}) %collective-permute-start) | collective-permute-done | bytes 393248 | tf_op jit(solution)/shard_map/while/body/eval_jaxpr/ppermute | solution.py:32
  693.9 12.5 %collective-permute-done = f32[3,16,16,128]{3,2,1,0:T(8,128)S(1)} collective-permute-done((f32[3,16,16,128]{3,2,1,0:T(8,128)S(1)}, f32[3,16,16,128]{3,2,1,0:T(8,128)S(1)}, u32[]{:S(2)}, u32[]{:S(2)}) %collective-permute-start) | collective-permute-done | bytes 393248 | tf_op jit(solution)/shard_map/while/body/eval_jaxpr/ppermute | solution.py:32
  708.5 11.6 %collective-permute-done = f32[3,16,16,128]{3,2,1,0:T(8,128)S(1)} collective-permute-done((f32[3,16,16,128]{3,2,1,0:T(8,128)S(1)}, f32[3,16,16,128]{3,2,1,0:T(8,128)S(1)}, u32[]{:S(2)}, u32[]{:S(2)}) %collective-permute-start) | collective-permute-done | bytes 393248 | tf_op jit(solution)/shard_map/while/body/eval_jaxpr/ppermute | solution.py:32
  760.6 11.0 %collective-permute-done = f32[3,16,16,128]{3,2,1,0:T(8,128)S(1)} collective-permute-done((f32[3,16,16,128]{3,2,1,0:T(8,128)S(1)}, f32[3,16,16,128]{3,2,1,0:T(8,128)S(1)}, u32[]{:S(2)}, u32[]{:S(2)}) %collective-permute-start) | collective-permute-done | bytes 393248 | tf_op jit(solution)/shard_map/while/body/eval_jaxpr/ppermute | solution.py:32
  773.6 12.0 %collective-permute-done = f32[3,16,16,128]{3,2,1,0:T(8,128)S(1)} collective-permute-done((f32[3,16,16,128]{3,2,1,0:T(8,128)S(1)}, f32[3,16,16,128]{3,2,1,0:T(8,128)S(1)}, u32[]{:S(2)}, u32[]{:S(2)}) %collective-permute-start) | collective-permute-done | bytes 393248 | tf_op jit(solution)/shard_map/while/body/eval_jaxpr/ppermute | solution.py:32
  787.8 13.1 %collective-permute-done = f32[3,16,16,128]{3,2,1,0:T(8,128)S(1)} collective-permute-done((f32[3,16,16,128]{3,2,1,0:T(8,128)S(1)}, f32[3,16,16,128]{3,2,1,0:T(8,128)S(1)}, u32[]{:S(2)}, u32[]{:S(2)}) %collective-permute-start) | collective-permute-done | bytes 393248 | tf_op jit(solution)/shard_map/while/body/eval_jaxpr/ppermute | solution.py:32
  802.9 14.3 %collective-permute-done = f32[3,16,16,128]{3,2,1,0:T(8,128)S(1)} collective-permute-done((f32[3,16,16,128]{3,2,1,0:T(8,128)S(1)}, f32[3,16,16,128]{3,2,1,0:T(8,128)S(1)}, u32[]{:S(2)}, u32[]{:S(2)}) %collective-permute-start) | collective-permute-done | bytes 393248 | tf_op jit(solution)/shard_map/while/body/eval_jaxpr/ppermute | solution.py:32
  819.3 14.5 %collective-permute-done = f32[3,16,16,128]{3,2,1,0:T(8,128)S(1)} collective-permute-done((f32[3,16,16,128]{3,2,1,0:T(8,128)S(1)}, f32[3,16,16,128]{3,2,1,0:T(8,128)S(1)}, u32[]{:S(2)}, u32[]{:S(2)}) %collective-permute-start) | collective-permute-done | bytes 393248 | tf_op jit(solution)/shard_map/while/body/eval_jaxpr/ppermute | solution.py:32
  835.8 13.7 %collective-permute-done = f32[3,16,16,128]{3,2,1,0:T(8,128)S(1)} collective-permute-done((f32[3,16,16,128]{3,2,1,0:T(8,128)S(1)}, f32[3,16,16,128]{3,2,1,0:T(8,128)S(1)}, u32[]{:S(2)}, u32[]{:S(2)}) %collective-permute-start) | collective-permute-done | bytes 393248 | tf_op jit(solution)/shard_map/while/body/eval_jaxpr/ppermute | solution.py:32
  851.6 12.8 %collective-permute-done = f32[3,16,16,128]{3,2,1,0:T(8,128)S(1)} collective-permute-done((f32[3,16,16,128]{3,2,1,0:T(8,128)S(1)}, f32[3,16,16,128]{3,2,1,0:T(8,128)S(1)}, u32[]{:S(2)}, u32[]{:S(2)}) %collective-permute-start) | collective-permute-done | bytes 393248 | tf_op jit(solution)/shard_map/while/body/eval_jaxpr/ppermute | solution.py:32
  866.4 11.9 %collective-permute-done = f32[3,16,16,128]{3,2,1,0:T(8,128)S(1)} collective-permute-done((f32[3,16,16,128]{3,2,1,0:T(8,128)S(1)}, f32[3,16,16,128]{3,2,1,0:T(8,128)S(1)}, u32[]{:S(2)}, u32[]{:S(2)}) %collective-permute-start) | collective-permute-done | bytes 393248 | tf_op jit(solution)/shard_map/while/body/eval_jaxpr/ppermute | solution.py:32
  (279 shorter events, 347.6 us)
Async XLA Ops:
  45.4 14.9 %collective-permute-start = (f32[3,16,16,128]{3,2,1,0:T(8,128)S(1)}, f32[3,16,16,128]{3,2,1,0:T(8,128)S(1)}, u32[]{:S(2)}, u32[]{:S(2)}) collective-permute-start(f32[3,16,16,128]{3,2,1,0:T(8,128)S(1)} %multiply_add_fusion.7), channel_id=1, source_target_pairs={{0,4},{4,8},{8,12},{12,16},{16,20},{20,24},{24,28},{28,32},{32,36}... | collective-permute-start | bytes 1179656 | tf_op jit(solution)/shard_map/while/body/eval_jaxpr/ppermute | solution.py:32
  60.4 13.4 %collective-permute-start = (f32[3,16,16,128]{3,2,1,0:T(8,128)S(1)}, f32[3,16,16,128]{3,2,1,0:T(8,128)S(1)}, u32[]{:S(2)}, u32[]{:S(2)}) collective-permute-start(f32[3,16,16,128]{3,2,1,0:T(8,128)S(1)} %multiply_add_fusion.7), channel_id=1, source_target_pairs={{0,4},{4,8},{8,12},{12,16},{16,20},{20,24},{24,28},{28,32},{32,36}... | collective-permute-start | bytes 1179656 | tf_op jit(solution)/shard_map/while/body/eval_jaxpr/ppermute | solution.py:32
  86.8 12.7 %collective-permute-start = (f32[3,16,16,128]{3,2,1,0:T(8,128)S(1)}, f32[3,16,16,128]{3,2,1,0:T(8,128)S(1)}, u32[]{:S(2)}, u32[]{:S(2)}) collective-permute-start(f32[3,16,16,128]{3,2,1,0:T(8,128)S(1)} %multiply_add_fusion.7), channel_id=1, source_target_pairs={{0,4},{4,8},{8,12},{12,16},{16,20},{20,24},{24,28},{28,32},{32,36}... | collective-permute-start | bytes 1179656 | tf_op jit(solution)/shard_map/while/body/eval_jaxpr/ppermute | solution.py:32
  112.4 13.0 %collective-permute-start = (f32[3,16,16,128]{3,2,1,0:T(8,128)S(1)}, f32[3,16,16,128]{3,2,1,0:T(8,128)S(1)}, u32[]{:S(2)}, u32[]{:S(2)}) collective-permute-start(f32[3,16,16,128]{3,2,1,0:T(8,128)S(1)} %multiply_add_fusion.7), channel_id=1, source_target_pairs={{0,4},{4,8},{8,12},{12,16},{16,20},{20,24},{24,28},{28,32},{32,36}... | collective-permute-start | bytes 1179656 | tf_op jit(solution)/shard_map/while/body/eval_jaxpr/ppermute | solution.py:32
  125.6 14.1 %collective-permute-start = (f32[3,16,16,128]{3,2,1,0:T(8,128)S(1)}, f32[3,16,16,128]{3,2,1,0:T(8,128)S(1)}, u32[]{:S(2)}, u32[]{:S(2)}) collective-permute-start(f32[3,16,16,128]{3,2,1,0:T(8,128)S(1)} %multiply_add_fusion.7), channel_id=1, source_target_pairs={{0,4},{4,8},{8,12},{12,16},{16,20},{20,24},{24,28},{28,32},{32,36}... | collective-permute-start | bytes 1179656 | tf_op jit(solution)/shard_map/while/body/eval_jaxpr/ppermute | solution.py:32
  139.8 15.2 %collective-permute-start = (f32[3,16,16,128]{3,2,1,0:T(8,128)S(1)}, f32[3,16,16,128]{3,2,1,0:T(8,128)S(1)}, u32[]{:S(2)}, u32[]{:S(2)}) collective-permute-start(f32[3,16,16,128]{3,2,1,0:T(8,128)S(1)} %multiply_add_fusion.7), channel_id=1, source_target_pairs={{0,4},{4,8},{8,12},{12,16},{16,20},{20,24},{24,28},{28,32},{32,36}... | collective-permute-start | bytes 1179656 | tf_op jit(solution)/shard_map/while/body/eval_jaxpr/ppermute | solution.py:32
  155.2 16.4 %collective-permute-start = (f32[3,16,16,128]{3,2,1,0:T(8,128)S(1)}, f32[3,16,16,128]{3,2,1,0:T(8,128)S(1)}, u32[]{:S(2)}, u32[]{:S(2)}) collective-permute-start(f32[3,16,16,128]{3,2,1,0:T(8,128)S(1)} %multiply_add_fusion.7), channel_id=1, source_target_pairs={{0,4},{4,8},{8,12},{12,16},{16,20},{20,24},{24,28},{28,32},{32,36}... | collective-permute-start | bytes 1179656 | tf_op jit(solution)/shard_map/while/body/eval_jaxpr/ppermute | solution.py:32
  171.7 16.2 %collective-permute-start = (f32[3,16,16,128]{3,2,1,0:T(8,128)S(1)}, f32[3,16,16,128]{3,2,1,0:T(8,128)S(1)}, u32[]{:S(2)}, u32[]{:S(2)}) collective-permute-start(f32[3,16,16,128]{3,2,1,0:T(8,128)S(1)} %multiply_add_fusion.7), channel_id=1, source_target_pairs={{0,4},{4,8},{8,12},{12,16},{16,20},{20,24},{24,28},{28,32},{32,36}... | collective-permute-start | bytes 1179656 | tf_op jit(solution)/shard_map/while/body/eval_jaxpr/ppermute | solution.py:32
  188.1 15.4 %collective-permute-start = (f32[3,16,16,128]{3,2,1,0:T(8,128)S(1)}, f32[3,16,16,128]{3,2,1,0:T(8,128)S(1)}, u32[]{:S(2)}, u32[]{:S(2)}) collective-permute-start(f32[3,16,16,128]{3,2,1,0:T(8,128)S(1)} %multiply_add_fusion.7), channel_id=1, source_target_pairs={{0,4},{4,8},{8,12},{12,16},{16,20},{20,24},{24,28},{28,32},{32,36}... | collective-permute-start | bytes 1179656 | tf_op jit(solution)/shard_map/while/body/eval_jaxpr/ppermute | solution.py:32
  203.6 14.5 %collective-permute-start = (f32[3,16,16,128]{3,2,1,0:T(8,128)S(1)}, f32[3,16,16,128]{3,2,1,0:T(8,128)S(1)}, u32[]{:S(2)}, u32[]{:S(2)}) collective-permute-start(f32[3,16,16,128]{3,2,1,0:T(8,128)S(1)} %multiply_add_fusion.7), channel_id=1, source_target_pairs={{0,4},{4,8},{8,12},{12,16},{16,20},{20,24},{24,28},{28,32},{32,36}... | collective-permute-start | bytes 1179656 | tf_op jit(solution)/shard_map/while/body/eval_jaxpr/ppermute | solution.py:32
  218.3 13.6 %collective-permute-start = (f32[3,16,16,128]{3,2,1,0:T(8,128)S(1)}, f32[3,16,16,128]{3,2,1,0:T(8,128)S(1)}, u32[]{:S(2)}, u32[]{:S(2)}) collective-permute-start(f32[3,16,16,128]{3,2,1,0:T(8,128)S(1)} %multiply_add_fusion.7), channel_id=1, source_target_pairs={{0,4},{4,8},{8,12},{12,16},{16,20},{20,24},{24,28},{28,32},{32,36}... | collective-permute-start | bytes 1179656 | tf_op jit(solution)/shard_map/while/body/eval_jaxpr/ppermute | solution.py:32
  232.0 12.7 %collective-permute-start = (f32[3,16,16,128]{3,2,1,0:T(8,128)S(1)}, f32[3,16,16,128]{3,2,1,0:T(8,128)S(1)}, u32[]{:S(2)}, u32[]{:S(2)}) collective-permute-start(f32[3,16,16,128]{3,2,1,0:T(8,128)S(1)} %multiply_add_fusion.7), channel_id=1, source_target_pairs={{0,4},{4,8},{8,12},{12,16},{16,20},{20,24},{24,28},{28,32},{32,36}... | collective-permute-start | bytes 1179656 | tf_op jit(solution)/shard_map/while/body/eval_jaxpr/ppermute | solution.py:32
  257.6 12.7 %collective-permute-start = (f32[3,16,16,128]{3,2,1,0:T(8,128)S(1)}, f32[3,16,16,128]{3,2,1,0:T(8,128)S(1)}, u32[]{:S(2)}, u32[]{:S(2)}) collective-permute-start(f32[3,16,16,128]{3,2,1,0:T(8,128)S(1)} %multiply_add_fusion.7), channel_id=1, source_target_pairs={{0,4},{4,8},{8,12},{12,16},{16,20},{20,24},{24,28},{28,32},{32,36}... | collective-permute-start | bytes 1179656 | tf_op jit(solution)/shard_map/while/body/eval_jaxpr/ppermute | solution.py:32
  270.4 12.9 %collective-permute-start = (f32[3,16,16,128]{3,2,1,0:T(8,128)S(1)}, f32[3,16,16,128]{3,2,1,0:T(8,128)S(1)}, u32[]{:S(2)}, u32[]{:S(2)}) collective-permute-start(f32[3,16,16,128]{3,2,1,0:T(8,128)S(1)} %multiply_add_fusion.7), channel_id=1, source_target_pairs={{0,4},{4,8},{8,12},{12,16},{16,20},{20,24},{24,28},{28,32},{32,36}... | collective-permute-start | bytes 1179656 | tf_op jit(solution)/shard_map/while/body/eval_jaxpr/ppermute | solution.py:32
  283.4 13.9 %collective-permute-start = (f32[3,16,16,128]{3,2,1,0:T(8,128)S(1)}, f32[3,16,16,128]{3,2,1,0:T(8,128)S(1)}, u32[]{:S(2)}, u32[]{:S(2)}) collective-permute-start(f32[3,16,16,128]{3,2,1,0:T(8,128)S(1)} %multiply_add_fusion.7), channel_id=1, source_target_pairs={{0,4},{4,8},{8,12},{12,16},{16,20},{20,24},{24,28},{28,32},{32,36}... | collective-permute-start | bytes 1179656 | tf_op jit(solution)/shard_map/while/body/eval_jaxpr/ppermute | solution.py:32
  297.5 15.0 %collective-permute-start = (f32[3,16,16,128]{3,2,1,0:T(8,128)S(1)}, f32[3,16,16,128]{3,2,1,0:T(8,128)S(1)}, u32[]{:S(2)}, u32[]{:S(2)}) collective-permute-start(f32[3,16,16,128]{3,2,1,0:T(8,128)S(1)} %multiply_add_fusion.7), channel_id=1, source_target_pairs={{0,4},{4,8},{8,12},{12,16},{16,20},{20,24},{24,28},{28,32},{32,36}... | collective-permute-start | bytes 1179656 | tf_op jit(solution)/shard_map/while/body/eval_jaxpr/ppermute | solution.py:32
  312.6 16.2 %collective-permute-start = (f32[3,16,16,128]{3,2,1,0:T(8,128)S(1)}, f32[3,16,16,128]{3,2,1,0:T(8,128)S(1)}, u32[]{:S(2)}, u32[]{:S(2)}) collective-permute-start(f32[3,16,16,128]{3,2,1,0:T(8,128)S(1)} %multiply_add_fusion.7), channel_id=1, source_target_pairs={{0,4},{4,8},{8,12},{12,16},{16,20},{20,24},{24,28},{28,32},{32,36}... | collective-permute-start | bytes 1179656 | tf_op jit(solution)/shard_map/while/body/eval_jaxpr/ppermute | solution.py:32
  328.9 16.4 %collective-permute-start = (f32[3,16,16,128]{3,2,1,0:T(8,128)S(1)}, f32[3,16,16,128]{3,2,1,0:T(8,128)S(1)}, u32[]{:S(2)}, u32[]{:S(2)}) collective-permute-start(f32[3,16,16,128]{3,2,1,0:T(8,128)S(1)} %multiply_add_fusion.7), channel_id=1, source_target_pairs={{0,4},{4,8},{8,12},{12,16},{16,20},{20,24},{24,28},{28,32},{32,36}... | collective-permute-start | bytes 1179656 | tf_op jit(solution)/shard_map/while/body/eval_jaxpr/ppermute | solution.py:32
  345.5 15.7 %collective-permute-start = (f32[3,16,16,128]{3,2,1,0:T(8,128)S(1)}, f32[3,16,16,128]{3,2,1,0:T(8,128)S(1)}, u32[]{:S(2)}, u32[]{:S(2)}) collective-permute-start(f32[3,16,16,128]{3,2,1,0:T(8,128)S(1)} %multiply_add_fusion.7), channel_id=1, source_target_pairs={{0,4},{4,8},{8,12},{12,16},{16,20},{20,24},{24,28},{28,32},{32,36}... | collective-permute-start | bytes 1179656 | tf_op jit(solution)/shard_map/while/body/eval_jaxpr/ppermute | solution.py:32
  361.3 14.8 %collective-permute-start = (f32[3,16,16,128]{3,2,1,0:T(8,128)S(1)}, f32[3,16,16,128]{3,2,1,0:T(8,128)S(1)}, u32[]{:S(2)}, u32[]{:S(2)}) collective-permute-start(f32[3,16,16,128]{3,2,1,0:T(8,128)S(1)} %multiply_add_fusion.7), channel_id=1, source_target_pairs={{0,4},{4,8},{8,12},{12,16},{16,20},{20,24},{24,28},{28,32},{32,36}... | collective-permute-start | bytes 1179656 | tf_op jit(solution)/shard_map/while/body/eval_jaxpr/ppermute | solution.py:32
  376.2 13.8 %collective-permute-start = (f32[3,16,16,128]{3,2,1,0:T(8,128)S(1)}, f32[3,16,16,128]{3,2,1,0:T(8,128)S(1)}, u32[]{:S(2)}, u32[]{:S(2)}) collective-permute-start(f32[3,16,16,128]{3,2,1,0:T(8,128)S(1)} %multiply_add_fusion.7), channel_id=1, source_target_pairs={{0,4},{4,8},{8,12},{12,16},{16,20},{20,24},{24,28},{28,32},{32,36}... | collective-permute-start | bytes 1179656 | tf_op jit(solution)/shard_map/while/body/eval_jaxpr/ppermute | solution.py:32
  390.2 12.9 %collective-permute-start = (f32[3,16,16,128]{3,2,1,0:T(8,128)S(1)}, f32[3,16,16,128]{3,2,1,0:T(8,128)S(1)}, u32[]{:S(2)}, u32[]{:S(2)}) collective-permute-start(f32[3,16,16,128]{3,2,1,0:T(8,128)S(1)} %multiply_add_fusion.7), channel_id=1, source_target_pairs={{0,4},{4,8},{8,12},{12,16},{16,20},{20,24},{24,28},{28,32},{32,36}... | collective-permute-start | bytes 1179656 | tf_op jit(solution)/shard_map/while/body/eval_jaxpr/ppermute | solution.py:32
  441.7 13.5 %collective-permute-start = (f32[3,16,16,128]{3,2,1,0:T(8,128)S(1)}, f32[3,16,16,128]{3,2,1,0:T(8,128)S(1)}, u32[]{:S(2)}, u32[]{:S(2)}) collective-permute-start(f32[3,16,16,128]{3,2,1,0:T(8,128)S(1)} %multiply_add_fusion.7), channel_id=1, source_target_pairs={{0,4},{4,8},{8,12},{12,16},{16,20},{20,24},{24,28},{28,32},{32,36}... | collective-permute-start | bytes 1179656 | tf_op jit(solution)/shard_map/while/body/eval_jaxpr/ppermute | solution.py:32
  455.3 14.6 %collective-permute-start = (f32[3,16,16,128]{3,2,1,0:T(8,128)S(1)}, f32[3,16,16,128]{3,2,1,0:T(8,128)S(1)}, u32[]{:S(2)}, u32[]{:S(2)}) collective-permute-start(f32[3,16,16,128]{3,2,1,0:T(8,128)S(1)} %multiply_add_fusion.7), channel_id=1, source_target_pairs={{0,4},{4,8},{8,12},{12,16},{16,20},{20,24},{24,28},{28,32},{32,36}... | collective-permute-start | bytes 1179656 | tf_op jit(solution)/shard_map/while/body/eval_jaxpr/ppermute | solution.py:32
  470.0 15.7 %collective-permute-start = (f32[3,16,16,128]{3,2,1,0:T(8,128)S(1)}, f32[3,16,16,128]{3,2,1,0:T(8,128)S(1)}, u32[]{:S(2)}, u32[]{:S(2)}) collective-permute-start(f32[3,16,16,128]{3,2,1,0:T(8,128)S(1)} %multiply_add_fusion.7), channel_id=1, source_target_pairs={{0,4},{4,8},{8,12},{12,16},{16,20},{20,24},{24,28},{28,32},{32,36}... | collective-permute-start | bytes 1179656 | tf_op jit(solution)/shard_map/while/body/eval_jaxpr/ppermute | solution.py:32
  485.9 16.9 %collective-permute-start = (f32[3,16,16,128]{3,2,1,0:T(8,128)S(1)}, f32[3,16,16,128]{3,2,1,0:T(8,128)S(1)}, u32[]{:S(2)}, u32[]{:S(2)}) collective-permute-start(f32[3,16,16,128]{3,2,1,0:T(8,128)S(1)} %multiply_add_fusion.7), channel_id=1, source_target_pairs={{0,4},{4,8},{8,12},{12,16},{16,20},{20,24},{24,28},{28,32},{32,36}... | collective-permute-start | bytes 1179656 | tf_op jit(solution)/shard_map/while/body/eval_jaxpr/ppermute | solution.py:32
  502.9 16.0 %collective-permute-start = (f32[3,16,16,128]{3,2,1,0:T(8,128)S(1)}, f32[3,16,16,128]{3,2,1,0:T(8,128)S(1)}, u32[]{:S(2)}, u32[]{:S(2)}) collective-permute-start(f32[3,16,16,128]{3,2,1,0:T(8,128)S(1)} %multiply_add_fusion.7), channel_id=1, source_target_pairs={{0,4},{4,8},{8,12},{12,16},{16,20},{20,24},{24,28},{28,32},{32,36}... | collective-permute-start | bytes 1179656 | tf_op jit(solution)/shard_map/while/body/eval_jaxpr/ppermute | solution.py:32
  519.0 15.2 %collective-permute-start = (f32[3,16,16,128]{3,2,1,0:T(8,128)S(1)}, f32[3,16,16,128]{3,2,1,0:T(8,128)S(1)}, u32[]{:S(2)}, u32[]{:S(2)}) collective-permute-start(f32[3,16,16,128]{3,2,1,0:T(8,128)S(1)} %multiply_add_fusion.7), channel_id=1, source_target_pairs={{0,4},{4,8},{8,12},{12,16},{16,20},{20,24},{24,28},{28,32},{32,36}... | collective-permute-start | bytes 1179656 | tf_op jit(solution)/shard_map/while/body/eval_jaxpr/ppermute | solution.py:32
  534.4 14.3 %collective-permute-start = (f32[3,16,16,128]{3,2,1,0:T(8,128)S(1)}, f32[3,16,16,128]{3,2,1,0:T(8,128)S(1)}, u32[]{:S(2)}, u32[]{:S(2)}) collective-permute-start(f32[3,16,16,128]{3,2,1,0:T(8,128)S(1)} %multiply_add_fusion.7), channel_id=1, source_target_pairs={{0,4},{4,8},{8,12},{12,16},{16,20},{20,24},{24,28},{28,32},{32,36}... | collective-permute-start | bytes 1179656 | tf_op jit(solution)/shard_map/while/body/eval_jaxpr/ppermute | solution.py:32
  548.8 13.4 %collective-permute-start = (f32[3,16,16,128]{3,2,1,0:T(8,128)S(1)}, f32[3,16,16,128]{3,2,1,0:T(8,128)S(1)}, u32[]{:S(2)}, u32[]{:S(2)}) collective-permute-start(f32[3,16,16,128]{3,2,1,0:T(8,128)S(1)} %multiply_add_fusion.7), channel_id=1, source_target_pairs={{0,4},{4,8},{8,12},{12,16},{16,20},{20,24},{24,28},{28,32},{32,36}... | collective-permute-start | bytes 1179656 | tf_op jit(solution)/shard_map/while/body/eval_jaxpr/ppermute | solution.py:32
  575.1 12.7 %collective-permute-start = (f32[3,16,16,128]{3,2,1,0:T(8,128)S(1)}, f32[3,16,16,128]{3,2,1,0:T(8,128)S(1)}, u32[]{:S(2)}, u32[]{:S(2)}) collective-permute-start(f32[3,16,16,128]{3,2,1,0:T(8,128)S(1)} %multiply_add_fusion.7), channel_id=1, source_target_pairs={{0,4},{4,8},{8,12},{12,16},{16,20},{20,24},{24,28},{28,32},{32,36}... | collective-permute-start | bytes 1179656 | tf_op jit(solution)/shard_map/while/body/eval_jaxpr/ppermute | solution.py:32
  600.7 13.1 %collective-permute-start = (f32[3,16,16,128]{3,2,1,0:T(8,128)S(1)}, f32[3,16,16,128]{3,2,1,0:T(8,128)S(1)}, u32[]{:S(2)}, u32[]{:S(2)}) collective-permute-start(f32[3,16,16,128]{3,2,1,0:T(8,128)S(1)} %multiply_add_fusion.7), channel_id=1, source_target_pairs={{0,4},{4,8},{8,12},{12,16},{16,20},{20,24},{24,28},{28,32},{32,36}... | collective-permute-start | bytes 1179656 | tf_op jit(solution)/shard_map/while/body/eval_jaxpr/ppermute | solution.py:32
  613.9 14.1 %collective-permute-start = (f32[3,16,16,128]{3,2,1,0:T(8,128)S(1)}, f32[3,16,16,128]{3,2,1,0:T(8,128)S(1)}, u32[]{:S(2)}, u32[]{:S(2)}) collective-permute-start(f32[3,16,16,128]{3,2,1,0:T(8,128)S(1)} %multiply_add_fusion.7), channel_id=1, source_target_pairs={{0,4},{4,8},{8,12},{12,16},{16,20},{20,24},{24,28},{28,32},{32,36}... | collective-permute-start | bytes 1179656 | tf_op jit(solution)/shard_map/while/body/eval_jaxpr/ppermute | solution.py:32
  628.2 15.2 %collective-permute-start = (f32[3,16,16,128]{3,2,1,0:T(8,128)S(1)}, f32[3,16,16,128]{3,2,1,0:T(8,128)S(1)}, u32[]{:S(2)}, u32[]{:S(2)}) collective-permute-start(f32[3,16,16,128]{3,2,1,0:T(8,128)S(1)} %multiply_add_fusion.7), channel_id=1, source_target_pairs={{0,4},{4,8},{8,12},{12,16},{16,20},{20,24},{24,28},{28,32},{32,36}... | collective-permute-start | bytes 1179656 | tf_op jit(solution)/shard_map/while/body/eval_jaxpr/ppermute | solution.py:32
  643.6 16.4 %collective-permute-start = (f32[3,16,16,128]{3,2,1,0:T(8,128)S(1)}, f32[3,16,16,128]{3,2,1,0:T(8,128)S(1)}, u32[]{:S(2)}, u32[]{:S(2)}) collective-permute-start(f32[3,16,16,128]{3,2,1,0:T(8,128)S(1)} %multiply_add_fusion.7), channel_id=1, source_target_pairs={{0,4},{4,8},{8,12},{12,16},{16,20},{20,24},{24,28},{28,32},{32,36}... | collective-permute-start | bytes 1179656 | tf_op jit(solution)/shard_map/while/body/eval_jaxpr/ppermute | solution.py:32
  660.1 16.2 %collective-permute-start = (f32[3,16,16,128]{3,2,1,0:T(8,128)S(1)}, f32[3,16,16,128]{3,2,1,0:T(8,128)S(1)}, u32[]{:S(2)}, u32[]{:S(2)}) collective-permute-start(f32[3,16,16,128]{3,2,1,0:T(8,128)S(1)} %multiply_add_fusion.7), channel_id=1, source_target_pairs={{0,4},{4,8},{8,12},{12,16},{16,20},{20,24},{24,28},{28,32},{32,36}... | collective-permute-start | bytes 1179656 | tf_op jit(solution)/shard_map/while/body/eval_jaxpr/ppermute | solution.py:32
  676.5 15.4 %collective-permute-start = (f32[3,16,16,128]{3,2,1,0:T(8,128)S(1)}, f32[3,16,16,128]{3,2,1,0:T(8,128)S(1)}, u32[]{:S(2)}, u32[]{:S(2)}) collective-permute-start(f32[3,16,16,128]{3,2,1,0:T(8,128)S(1)} %multiply_add_fusion.7), channel_id=1, source_target_pairs={{0,4},{4,8},{8,12},{12,16},{16,20},{20,24},{24,28},{28,32},{32,36}... | collective-permute-start | bytes 1179656 | tf_op jit(solution)/shard_map/while/body/eval_jaxpr/ppermute | solution.py:32
  692.0 14.5 %collective-permute-start = (f32[3,16,16,128]{3,2,1,0:T(8,128)S(1)}, f32[3,16,16,128]{3,2,1,0:T(8,128)S(1)}, u32[]{:S(2)}, u32[]{:S(2)}) collective-permute-start(f32[3,16,16,128]{3,2,1,0:T(8,128)S(1)} %multiply_add_fusion.7), channel_id=1, source_target_pairs={{0,4},{4,8},{8,12},{12,16},{16,20},{20,24},{24,28},{28,32},{32,36}... | collective-permute-start | bytes 1179656 | tf_op jit(solution)/shard_map/while/body/eval_jaxpr/ppermute | solution.py:32
  706.6 13.5 %collective-permute-start = (f32[3,16,16,128]{3,2,1,0:T(8,128)S(1)}, f32[3,16,16,128]{3,2,1,0:T(8,128)S(1)}, u32[]{:S(2)}, u32[]{:S(2)}) collective-permute-start(f32[3,16,16,128]{3,2,1,0:T(8,128)S(1)} %multiply_add_fusion.7), channel_id=1, source_target_pairs={{0,4},{4,8},{8,12},{12,16},{16,20},{20,24},{24,28},{28,32},{32,36}... | collective-permute-start | bytes 1179656 | tf_op jit(solution)/shard_map/while/body/eval_jaxpr/ppermute | solution.py:32
  745.9 12.7 %collective-permute-start = (f32[3,16,16,128]{3,2,1,0:T(8,128)S(1)}, f32[3,16,16,128]{3,2,1,0:T(8,128)S(1)}, u32[]{:S(2)}, u32[]{:S(2)}) collective-permute-start(f32[3,16,16,128]{3,2,1,0:T(8,128)S(1)} %multiply_add_fusion.7), channel_id=1, source_target_pairs={{0,4},{4,8},{8,12},{12,16},{16,20},{20,24},{24,28},{28,32},{32,36}... | collective-permute-start | bytes 1179656 | tf_op jit(solution)/shard_map/while/body/eval_jaxpr/ppermute | solution.py:32
  758.7 12.9 %collective-permute-start = (f32[3,16,16,128]{3,2,1,0:T(8,128)S(1)}, f32[3,16,16,128]{3,2,1,0:T(8,128)S(1)}, u32[]{:S(2)}, u32[]{:S(2)}) collective-permute-start(f32[3,16,16,128]{3,2,1,0:T(8,128)S(1)} %multiply_add_fusion.7), channel_id=1, source_target_pairs={{0,4},{4,8},{8,12},{12,16},{16,20},{20,24},{24,28},{28,32},{32,36}... | collective-permute-start | bytes 1179656 | tf_op jit(solution)/shard_map/while/body/eval_jaxpr/ppermute | solution.py:32
  771.7 14.0 %collective-permute-start = (f32[3,16,16,128]{3,2,1,0:T(8,128)S(1)}, f32[3,16,16,128]{3,2,1,0:T(8,128)S(1)}, u32[]{:S(2)}, u32[]{:S(2)}) collective-permute-start(f32[3,16,16,128]{3,2,1,0:T(8,128)S(1)} %multiply_add_fusion.7), channel_id=1, source_target_pairs={{0,4},{4,8},{8,12},{12,16},{16,20},{20,24},{24,28},{28,32},{32,36}... | collective-permute-start | bytes 1179656 | tf_op jit(solution)/shard_map/while/body/eval_jaxpr/ppermute | solution.py:32
  785.8 15.0 %collective-permute-start = (f32[3,16,16,128]{3,2,1,0:T(8,128)S(1)}, f32[3,16,16,128]{3,2,1,0:T(8,128)S(1)}, u32[]{:S(2)}, u32[]{:S(2)}) collective-permute-start(f32[3,16,16,128]{3,2,1,0:T(8,128)S(1)} %multiply_add_fusion.7), channel_id=1, source_target_pairs={{0,4},{4,8},{8,12},{12,16},{16,20},{20,24},{24,28},{28,32},{32,36}... | collective-permute-start | bytes 1179656 | tf_op jit(solution)/shard_map/while/body/eval_jaxpr/ppermute | solution.py:32
  801.0 16.2 %collective-permute-start = (f32[3,16,16,128]{3,2,1,0:T(8,128)S(1)}, f32[3,16,16,128]{3,2,1,0:T(8,128)S(1)}, u32[]{:S(2)}, u32[]{:S(2)}) collective-permute-start(f32[3,16,16,128]{3,2,1,0:T(8,128)S(1)} %multiply_add_fusion.7), channel_id=1, source_target_pairs={{0,4},{4,8},{8,12},{12,16},{16,20},{20,24},{24,28},{28,32},{32,36}... | collective-permute-start | bytes 1179656 | tf_op jit(solution)/shard_map/while/body/eval_jaxpr/ppermute | solution.py:32
  817.4 16.4 %collective-permute-start = (f32[3,16,16,128]{3,2,1,0:T(8,128)S(1)}, f32[3,16,16,128]{3,2,1,0:T(8,128)S(1)}, u32[]{:S(2)}, u32[]{:S(2)}) collective-permute-start(f32[3,16,16,128]{3,2,1,0:T(8,128)S(1)} %multiply_add_fusion.7), channel_id=1, source_target_pairs={{0,4},{4,8},{8,12},{12,16},{16,20},{20,24},{24,28},{28,32},{32,36}... | collective-permute-start | bytes 1179656 | tf_op jit(solution)/shard_map/while/body/eval_jaxpr/ppermute | solution.py:32
  833.9 15.6 %collective-permute-start = (f32[3,16,16,128]{3,2,1,0:T(8,128)S(1)}, f32[3,16,16,128]{3,2,1,0:T(8,128)S(1)}, u32[]{:S(2)}, u32[]{:S(2)}) collective-permute-start(f32[3,16,16,128]{3,2,1,0:T(8,128)S(1)} %multiply_add_fusion.7), channel_id=1, source_target_pairs={{0,4},{4,8},{8,12},{12,16},{16,20},{20,24},{24,28},{28,32},{32,36}... | collective-permute-start | bytes 1179656 | tf_op jit(solution)/shard_map/while/body/eval_jaxpr/ppermute | solution.py:32
  849.7 14.7 %collective-permute-start = (f32[3,16,16,128]{3,2,1,0:T(8,128)S(1)}, f32[3,16,16,128]{3,2,1,0:T(8,128)S(1)}, u32[]{:S(2)}, u32[]{:S(2)}) collective-permute-start(f32[3,16,16,128]{3,2,1,0:T(8,128)S(1)} %multiply_add_fusion.7), channel_id=1, source_target_pairs={{0,4},{4,8},{8,12},{12,16},{16,20},{20,24},{24,28},{28,32},{32,36}... | collective-permute-start | bytes 1179656 | tf_op jit(solution)/shard_map/while/body/eval_jaxpr/ppermute | solution.py:32
  864.5 13.8 %collective-permute-start = (f32[3,16,16,128]{3,2,1,0:T(8,128)S(1)}, f32[3,16,16,128]{3,2,1,0:T(8,128)S(1)}, u32[]{:S(2)}, u32[]{:S(2)}) collective-permute-start(f32[3,16,16,128]{3,2,1,0:T(8,128)S(1)} %multiply_add_fusion.7), channel_id=1, source_target_pairs={{0,4},{4,8},{8,12},{12,16},{16,20},{20,24},{24,28},{28,32},{32,36}... | collective-permute-start | bytes 1179656 | tf_op jit(solution)/shard_map/while/body/eval_jaxpr/ppermute | solution.py:32
  (30 other events, 244.5 us)
where the time goes:
time: 946 us; the launch traced here: 943 us
  waiting for transfers between devices  787 us (83%)
  starting transfers between devices  135 us (14%)
  other arithmetic  12 us (1%)
    ppermute x63, waiting for transfers between devices, passed_along(): lax.ppermute(value, axis, [(source, source + steps) for source in range(f...  765 us
    ppermute x63, starting transfers between devices, passed_along(): lax.ppermute(value, axis, [(source, source + steps) for source in range(f...  123 us
  transfers between devices with their start and end apart: 75, of which 73 were waited for; matrix products, arithmetic and copies ran while one was open for 0% of the time, Pallas kernels for 0%

commit v1 on v0

v1 whole, which is shorter than its diff:
```python
import jax
import jax.numpy as jnp
from jax import lax
from jax.experimental import pallas as pl
from jax.experimental.pallas import tpu as pltpu
from jax.sharding import PartitionSpec as P

STEPS = 2
VISCOSITY = 0.05
TIME_STEP = 0.2
SLICES = 64
RING = 8
ROWS = 8
SLABS = 4
WIDE = 3 * STEPS
OWN = 16
SPAN = OWN + 2 * WIDE
GROUPS = 4
MESH = pl.DeviceIdType.MESH

KEEP = 1.0 - 6.0 * VISCOSITY * TIME_STEP
NEAR = VISCOSITY * TIME_STEP
HALF = 0.5 * TIME_STEP
WEIGHTS = ((0.0, 1.0), (0.75, 0.25), (1.0 / 3.0, 2.0 / 3.0))


def stage_plane(kind, src, base, plane, put):
    old, new = WEIGHTS[kind]
    row = lax.broadcasted_iota(jnp.int32, (8, 128), 0)
    first, last = row == 0, row == 7
    tile = 2 * plane
    core = [[src[c, tile + h] for h in range(2)] for c in range(3)]
    wind = [[core[c][h] * (new * HALF) for h in range(2)] for c in range(3)]
    for c in range(3):
        a, b = core[c]
        ra, rb = pltpu.roll(a, 1, 0), pltpu.roll(b, 1, 0)
        la, lb = pltpu.roll(a, 7, 0), pltpu.roll(b, 7, 0)
        before = (jnp.where(first, rb, ra), jnp.where(first, ra, rb))
        after = (jnp.where(last, lb, la), jnp.where(last, la, lb))
        for h in range(2):
            v = core[c][h]
            xm, xp = pltpu.roll(v, 1, 1), pltpu.roll(v, 127, 1)
            zm, zp = src[c, tile + h - 2], src[c, tile + h + 2]
            near = (xp + xm) + (after[h] + before[h]) + (zp + zm)
            advect = wind[0][h] * (xp - xm) + wind[1][h] * (after[h] - before[h]) + wind[2][h] * (zp - zm)
            out = (new * KEEP) * v + ((new * NEAR) * near - advect)
            if kind:
                out = out + old * base[c, tile + h]
            put(c, h, out)


def kernel(states, rate, out, w0, w1, w2, w3, w4, w5, jump, got, total, tots, path,
           load_sem, halo_send, halo_recv, up_send, up_recv, row_send, row_recv, down_send, down_recv, own_sem):
    tm, gz = lax.axis_index("tm"), lax.axis_index("gz")
    zi, row = lax.rem(tm, RING), lax.div(tm, RING)
    above, below = lax.rem(gz + 1, SLABS), lax.rem(gz + SLABS - 1, SLABS)
    far = lax.rem(gz, 2)
    start = row * RING

    barrier = pltpu.get_barrier_semaphore()
    for peer in (above, below):
        pl.semaphore_signal(barrier, inc=1, device_id={"gz": peer}, device_id_type=MESH)
    for q in range(1, RING):
        pl.semaphore_signal(barrier, inc=1, device_id={"tm": start + lax.rem(zi + q, RING)}, device_id_type=MESH)

    def greet(q, carry):
        pl.semaphore_signal(barrier, inc=1, device_id={"tm": q * RING + zi}, device_id_type=MESH)
        return carry

    lax.fori_loop(0, row, greet, 0)
    load = pltpu.make_async_copy(states, w0.at[:, pl.ds(2 * WIDE, 2 * OWN)], load_sem)
    load.start()
    pl.semaphore_wait(barrier, 2 + (RING - 1) + (ROWS - 1 - row))

    down_halo = pltpu.make_async_remote_copy(
        states.at[:, pl.ds(0, 2 * WIDE)], w0.at[:, pl.ds(2 * (OWN + WIDE), 2 * WIDE)], halo_send.at[0], halo_recv.at[1],
        device_id={"gz": below}, device_id_type=MESH)
    up_halo = pltpu.make_async_remote_copy(
        states.at[:, pl.ds(2 * (OWN - WIDE), 2 * WIDE)], w0.at[:, pl.ds(0, 2 * WIDE)], halo_send.at[1], halo_recv.at[0],
        device_id={"gz": above}, device_id_type=MESH)
    down_halo.start()
    up_halo.start()

    @pl.when(tm == 0)
    def _():
        pltpu.make_async_copy(states, out, own_sem.at[0]).start()

    works = (w0, w1, w2, w3, w4, w5)
    keep_own = jnp.where(tm == 0, 0.0, 1.0)

    def stages(first_plane, count, shift):
        for k in range(1, 2 * 3 + 1):
            src, base = works[k - 1], works[3 * ((k - 1) // 3)]
            kind = (k - 1) % 3
            begin = first_plane(k)

            def plane_turn(i, carry, k=k, src=src, base=base, kind=kind, begin=begin):
                plane = begin + i
                if k < 6:
                    def put(c, h, value):
                        works[k][c, 2 * plane + h] = value
                else:
                    damp = [jnp.exp(rate[2 * (plane - WIDE) + h] * (-1.0 / SLICES)) * keep_own for h in range(2)]

                    def put(c, h, value):
                        jump[c, 2 * (plane - WIDE) + h] = value - damp[h] * w0[c, 2 * plane + h]

                stage_plane(kind, src, base, plane, put)
                return carry

            lax.fori_loop(0, count(k), plane_turn, 0)

    bases = (6, 10 - 8 * far, 2 + 8 * far)

    def tile_of(group, k):
        if group < 3:
            return 2 * bases[group] + k
        return k + jnp.where(k >= 4, 24, 0)

    def send_up(group):
        for q in (4, 3, 5, 2, 6, 1, 7):
            peer = lax.rem(zi + q, RING)
            pltpu.make_async_remote_copy(
                jump.at[:, tile_of(group, peer)], got.at[group, zi], up_send.at[group], up_recv.at[group],
                device_id={"tm": start + peer}, device_id_type=MESH).start()

    def all_of(buf, send, recv):
        return pltpu.make_async_remote_copy(
            buf.at[pl.ds(0, RING - 1)], buf.at[pl.ds(0, RING - 1)], send, recv,
            device_id={"tm": tm}, device_id_type=MESH)

    def damp_of(group):
        return jnp.exp(rate[tile_of(group, zi)] * (-1.0 / SLICES))

    def sum_row(group):
        all_of(got.at[group], up_send.at[group], up_recv.at[group]).wait_recv()
        mine = tile_of(group, zi)
        for c in range(3):
            got[group, zi, c] = jump[c, mine]
        damp = damp_of(group)
        acc = [got[group, 0, c] for c in range(3)]
        for z in range(1, RING):
            acc = [damp * acc[c] + got[group, z, c] for c in range(3)]
        for c in range(3):
            total[group, c] = acc[c]

        def tell(later, carry):
            pltpu.make_async_remote_copy(
                total.at[group], tots.at[group, row], row_send.at[group, later], row_recv.at[group, row],
                device_id={"tm": later * RING + zi}, device_id_type=MESH).start()
            return carry

        lax.fori_loop(row + 1, ROWS, tell, 0)

    def send_down(group):
        damp = damp_of(group)
        eighth = damp * damp
        eighth = eighth * eighth
        eighth = eighth * eighth

        def add(q, carry):
            pltpu.make_async_remote_copy(
                total.at[group], tots.at[group, q], row_send.at[group, q], row_recv.at[group, q],
                device_id={"tm": q * RING + zi}, device_id_type=MESH).wait_recv()
            return tuple(eighth * carry[c] + tots[group, q, c] for c in range(3))

        acc = lax.fori_loop(0, row, add, tuple(jnp.zeros((8, 128), jnp.float32) for _ in range(3)))
        for z in range(RING):
            for c in range(3):
                path[group, z, c] = acc[c]
            if z < RING - 1:
                acc = [damp * acc[c] + got[group, z, c] for c in range(3)]
        mine = tile_of(group, zi)
        for q in (4, 3, 5, 2, 6, 1, 7):
            peer = lax.rem(zi + q, RING)

            @pl.when(start + peer > 0)
            def _():
                pltpu.make_async_remote_copy(
                    path.at[group, peer], out.at[:, mine], down_send.at[group, q], down_recv.at[group, q],
                    device_id={"tm": start + peer}, device_id_type=MESH).start()

        @pl.when(tm > 0)
        def _():
            pltpu.make_async_copy(path.at[group, zi], out.at[:, mine], own_sem.at[group]).start()

    load.wait()
    stages(lambda k: WIDE + k, lambda k: OWN - 2 * k, 0)
    send_up(0)

    def side(upper):
        @pl.when(upper == 0)
        def _():
            up_halo.wait_recv()

        @pl.when(upper == 1)
        def _():
            down_halo.wait_recv()

        stages(lambda k: jnp.where(upper == 1, OWN + WIDE - k, k), lambda k: WIDE, 0)

    side(1 - far)
    send_up(1)
    side(far)
    send_up(2)
    send_up(3)
    sum_row(0)
    sum_row(1)
    send_down(0)
    sum_row(2)
    send_down(1)
    sum_row(3)
    send_down(2)
    send_down(3)

    for group in range(GROUPS):
        mine = tile_of(group, zi)
        all_of(got.at[group], up_send.at[group], up_recv.at[group]).wait_send()

        def told(later, carry, group=group):
            pltpu.make_async_remote_copy(
                total.at[group], tots.at[group, row], row_send.at[group, later], row_recv.at[group, row],
                device_id={"tm": later * RING + zi}, device_id_type=MESH).wait_send()
            return carry

        lax.fori_loop(row + 1, ROWS, told, 0)
        for q in range(1, RING):
            peer, source = lax.rem(zi + q, RING), lax.rem(zi + RING - q, RING)

            @pl.when(start + peer > 0)
            def _():
                pltpu.make_async_remote_copy(
                    path.at[group, peer], out.at[:, mine], down_send.at[group, q], down_recv.at[group, q],
                    device_id={"tm": start + peer}, device_id_type=MESH).wait_send()

            @pl.when(tm > 0)
            def _():
                pltpu.make_async_remote_copy(
                    path.at[group, zi], out.at[:, tile_of(group, source)], down_send.at[group, q], down_recv.at[group, q],
                    device_id={"tm": start + source}, device_id_type=MESH).wait_recv()

        @pl.when(tm > 0)
        def _():
            pltpu.make_async_copy(path.at[group, zi], out.at[:, mine], own_sem.at[group]).wait()

    @pl.when(tm == 0)
    def _():
        pltpu.make_async_copy(states, out, own_sem.at[0]).wait()

    down_halo.wait_send()
    up_halo.wait_send()


def shards(states, rate):
    f32 = jnp.float32
    work = pltpu.VMEM((3, 2 * SPAN, 8, 128), f32)
    dma = pltpu.SemaphoreType.DMA
    out = pl.pallas_call(
        kernel,
        out_shape=jax.ShapeDtypeStruct((3, 2 * OWN, 8, 128), f32),
        in_specs=[pl.BlockSpec(memory_space=pl.ANY), pl.BlockSpec(memory_space=pltpu.VMEM)],
        out_specs=pl.BlockSpec(memory_space=pl.ANY),
        scratch_shapes=[work] * 6 + [
            pltpu.VMEM((3, 2 * OWN, 8, 128), f32),
            pltpu.VMEM((GROUPS, RING, 3, 8, 128), f32),
            pltpu.VMEM((GROUPS, 3, 8, 128), f32),
            pltpu.VMEM((GROUPS, ROWS, 3, 8, 128), f32),
            pltpu.VMEM((GROUPS, RING, 3, 8, 128), f32),
            dma, dma((2,)), dma((2,)), dma((GROUPS,)), dma((GROUPS,)),
            dma((GROUPS, ROWS)), dma((GROUPS, ROWS)), dma((GROUPS, RING)), dma((GROUPS, RING)), dma((GROUPS,)),
        ],
        compiler_params=pltpu.CompilerParams(collective_id=0, has_side_effects=True, vmem_limit_bytes=32 * 1024 * 1024),
    )(states.reshape(3, 2 * OWN, 8, 128), rate.reshape(2 * OWN, 8, 128))
    return out.reshape(1, 3, OWN, 16, 128)


def solution(mesh):
    return jax.shard_map(
        shards,
        mesh=mesh,
        in_specs=(P("tm", None, "gz", None, None), P("gz", None, None)),
        out_specs=P("tm", None, "gz", None, None),
        check_vma=False,
    )
```

time: 946 us -> 39.4 us (0.04)
  the two profiles are of different devices: /device:TPU:6 before, /device:TPU:28 now
where the time goes in v1:
time: 39.4 us; the launch traced here: 39.3 us
  Pallas kernels  36.6 us (93%)
  local copies, waits for them, and re-layouts  2.65 us (7%)
    pallas_call x1, Pallas kernels, shards(): pl.pallas_call(kernel, out_shape=jax.ShapeDtypeStruct((3, 2 * OWN, 8, 128...  36.6 us
    unnamed x5, local copies, waits for them, and re-layouts  2.65 us

profile of v1, /device:TPU:28, one launch (start us, length us, event | category | flops | bytes accessed | tf_op | source)
XLA Modules:
  0.0 39.3 jit_solution(528519426117840460)
XLA Ops:
  0.0 0.0 copy-start
  0.0 1.0 %copy-done = f32[1,3,16,16,128]{4,3,2,1,0:T(8,128)S(1)} copy-done((f32[1,3,16,16,128]{4,3,2,1,0:T(8,128)S(1)}, f32[1,3,16,16,128]{4,3,2,1,0:T(8,128)}, u32[]{:S(2)}) %copy-start) | copy-done | bytes 393240
  1.0 0.0 copy-start.1
  1.0 0.9 %copy-done.1 = f32[16,16,128]{2,1,0:T(8,128)S(1)} copy-done((f32[16,16,128]{2,1,0:T(8,128)S(1)}, f32[16,16,128]{2,1,0:T(8,128)}, u32[]{:S(2)}) %copy-start.1) | copy-done | bytes 131096
  1.9 36.6 %shard_map.28 = f32[3,32,8,128]{3,2,1,0:T(8,128)S(1)} custom-call(f32[3,32,8,128]{3,2,1,0:T(8,128)S(1)} %bitcast.4, f32[32,8,128]{2,1,0:T(8,128)S(1)} %bitcast.5), custom_call_target="tpu_custom_call" | custom-call | tf_op jit(solution)/shard_map/pallas_call | solution.py:258
  38.5 0.7 %copy.4 = f32[1,3,16,16,128]{4,3,2,1,0:T(8,128)} copy(f32[1,3,16,16,128]{4,3,2,1,0:T(8,128)S(1)} %bitcast.3) | data formatting | bytes 786432
Async XLA Ops:
  0.0 1.0 %copy-start = (f32[1,3,16,16,128]{4,3,2,1,0:T(8,128)S(1)}, f32[1,3,16,16,128]{4,3,2,1,0:T(8,128)}, u32[]{:S(2)}) copy-start(f32[1,3,16,16,128]{4,3,2,1,0:T(8,128)} %param.2) | copy-start | bytes 1179652
  1.0 0.9 %copy-start.1 = (f32[16,16,128]{2,1,0:T(8,128)S(1)}, f32[16,16,128]{2,1,0:T(8,128)}, u32[]{:S(2)}) copy-start(f32[16,16,128]{2,1,0:T(8,128)} %param.3) | copy-start | bytes 393220

commit v2 on v1

--- a/solution.py
+++ b/solution.py
@@ -49,7 +49,7 @@
             put(c, h, out)
 
 
-def kernel(states, rate, out, w0, w1, w2, w3, w4, w5, jump, got, total, tots, path,
+def kernel(states, rate_in, out, rate, w0, w1, w2, w3, w4, w5, jump, got, total, tots, path,
            load_sem, halo_send, halo_recv, up_send, up_recv, row_send, row_recv, down_send, down_recv, own_sem):
     tm, gz = lax.axis_index("tm"), lax.axis_index("gz")
     zi, row = lax.rem(tm, RING), lax.div(tm, RING)
@@ -57,6 +57,10 @@
     far = lax.rem(gz, 2)
     start = row * RING
 
+    load = pltpu.make_async_copy(states, w0.at[:, pl.ds(2 * WIDE, 2 * OWN)], load_sem.at[0])
+    load.start()
+    load_rate = pltpu.make_async_copy(rate_in, rate, load_sem.at[1])
+    load_rate.start()
     barrier = pltpu.get_barrier_semaphore()
     for peer in (above, below):
         pl.semaphore_signal(barrier, inc=1, device_id={"gz": peer}, device_id_type=MESH)
@@ -68,8 +72,6 @@
         return carry
 
     lax.fori_loop(0, row, greet, 0)
-    load = pltpu.make_async_copy(states, w0.at[:, pl.ds(2 * WIDE, 2 * OWN)], load_sem)
-    load.start()
     pl.semaphore_wait(barrier, 2 + (RING - 1) + (ROWS - 1 - row))
 
     down_halo = pltpu.make_async_remote_copy(
@@ -185,6 +187,7 @@
             pltpu.make_async_copy(path.at[group, zi], out.at[:, mine], own_sem.at[group]).start()
 
     load.wait()
+    load_rate.wait()
     stages(lambda k: WIDE + k, lambda k: OWN - 2 * k, 0)
     send_up(0)
 
@@ -258,19 +261,19 @@
     out = pl.pallas_call(
         kernel,
         out_shape=jax.ShapeDtypeStruct((3, 2 * OWN, 8, 128), f32),
-        in_specs=[pl.BlockSpec(memory_space=pl.ANY), pl.BlockSpec(memory_space=pltpu.VMEM)],
+        in_specs=[pl.BlockSpec(memory_space=pltpu.HBM), pl.BlockSpec(memory_space=pltpu.HBM)],
         out_specs=pl.BlockSpec(memory_space=pl.ANY),
-        scratch_shapes=[work] * 6 + [
+        scratch_shapes=[pltpu.VMEM((2 * OWN, 8, 128), f32)] + [work] * 6 + [
             pltpu.VMEM((3, 2 * OWN, 8, 128), f32),
             pltpu.VMEM((GROUPS, RING, 3, 8, 128), f32),
             pltpu.VMEM((GROUPS, 3, 8, 128), f32),
             pltpu.VMEM((GROUPS, ROWS, 3, 8, 128), f32),
             pltpu.VMEM((GROUPS, RING, 3, 8, 128), f32),
-            dma, dma((2,)), dma((2,)), dma((GROUPS,)), dma((GROUPS,)),
+            dma((2,)), dma((2,)), dma((2,)), dma((GROUPS,)), dma((GROUPS,)),
             dma((GROUPS, ROWS)), dma((GROUPS, ROWS)), dma((GROUPS, RING)), dma((GROUPS, RING)), dma((GROUPS,)),
         ],
         compiler_params=pltpu.CompilerParams(collective_id=0, has_side_effects=True, vmem_limit_bytes=32 * 1024 * 1024),
-    )(states.reshape(3, 2 * OWN, 8, 128), rate.reshape(2 * OWN, 8, 128))
+    )(pltpu.with_memory_space_constraint(states.reshape(3, 2 * OWN, 8, 128), pltpu.HBM), pltpu.with_memory_space_constraint(rate.reshape(2 * OWN, 8, 128), pltpu.HBM))
     return out.reshape(1, 3, OWN, 16, 128)
 
 

time: 39.4 us -> 36.7 us (0.931)
  the two profiles are of different devices: /device:TPU:28 before, /device:TPU:6 now
where the time goes in v2:
time: 36.7 us; the launch traced here: 36.6 us
  Pallas kernels  35.9 us (98%)
  local copies, waits for them, and re-layouts  0.75 us (2%)
    pallas_call x1, Pallas kernels, shards(): pl.pallas_call(kernel, out_shape=jax.ShapeDtypeStruct((3, 2 * OWN, 8, 128...  35.9 us
    unnamed x1, local copies, waits for them, and re-layouts  0.75 us

profile of v2, /device:TPU:6, one launch (start us, length us, event | category | flops | bytes accessed | tf_op | source)
XLA Modules:
  0.0 36.6 jit_solution(12107348266665746445)
XLA Ops:
  0.0 35.9 %shard_map.28 = f32[3,32,8,128]{3,2,1,0:T(8,128)S(1)} custom-call(f32[3,32,8,128]{3,2,1,0:T(8,128)} %bitcast.4, f32[32,8,128]{2,1,0:T(8,128)} %bitcast.5), custom_call_target="tpu_custom_call" | custom-call | tf_op jit(solution)/shard_map/pallas_call | solution.py:261
  35.9 0.7 %copy.4 = f32[1,3,16,16,128]{4,3,2,1,0:T(8,128)} copy(f32[1,3,16,16,128]{4,3,2,1,0:T(8,128)S(1)} %bitcast.3) | data formatting | bytes 786432

commit v3 on v2

--- a/solution.py
+++ b/solution.py
@@ -90,14 +90,13 @@
     works = (w0, w1, w2, w3, w4, w5)
     keep_own = jnp.where(tm == 0, 0.0, 1.0)
 
-    def stages(first_plane, count, shift):
+    def stages(first_plane, count, at_once):
         for k in range(1, 2 * 3 + 1):
             src, base = works[k - 1], works[3 * ((k - 1) // 3)]
             kind = (k - 1) % 3
             begin = first_plane(k)
 
-            def plane_turn(i, carry, k=k, src=src, base=base, kind=kind, begin=begin):
-                plane = begin + i
+            def one_plane(plane, k, src, base, kind):
                 if k < 6:
                     def put(c, h, value):
                         works[k][c, 2 * plane + h] = value
@@ -108,9 +107,17 @@
                         jump[c, 2 * (plane - WIDE) + h] = value - damp[h] * w0[c, 2 * plane + h]
 
                 stage_plane(kind, src, base, plane, put)
+
+            def turn(i, carry, k=k, src=src, base=base, kind=kind, begin=begin):
+                for j in range(at_once[k - 1]):
+                    one_plane(begin + at_once[k - 1] * i + j, k, src, base, kind)
                 return carry
 
-            lax.fori_loop(0, count(k), plane_turn, 0)
+            turns = count(k) // at_once[k - 1]
+            if turns == 1:
+                turn(0, 0)
+            else:
+                lax.fori_loop(0, turns, turn, 0)
 
     bases = (6, 10 - 8 * far, 2 + 8 * far)
 
@@ -188,7 +195,7 @@
 
     load.wait()
     load_rate.wait()
-    stages(lambda k: WIDE + k, lambda k: OWN - 2 * k, 0)
+    stages(lambda k: WIDE + k, lambda k: OWN - 2 * k, (7, 6, 5, 8, 6, 4))
     send_up(0)
 
     def side(upper):
@@ -200,7 +207,7 @@
         def _():
             down_halo.wait_recv()
 
-        stages(lambda k: jnp.where(upper == 1, OWN + WIDE - k, k), lambda k: WIDE, 0)
+        stages(lambda k: jnp.where(upper == 1, OWN + WIDE - k, k), lambda k: WIDE, (6,) * 6)
 
     side(1 - far)
     send_up(1)

time: 36.7 us -> 32.3 us (0.88); the launches traced: 36.6 us -> 31.7 us
  Pallas kernels: 35.9 us -> 30.9 us
    pallas_call x1, Pallas kernels: 35.9 us -> 30.9 us  [shards(): pl.pallas_call(kernel, out_shape=jax.ShapeDtypeStruct((3, 2 * OWN, 8, 128...]
where the time goes in v3:
time: 32.3 us; the launch traced here: 31.7 us
  Pallas kernels  30.9 us (96%)
  local copies, waits for them, and re-layouts  0.75 us (2%)
    pallas_call x1, Pallas kernels, shards(): pl.pallas_call(kernel, out_shape=jax.ShapeDtypeStruct((3, 2 * OWN, 8, 128...  30.9 us
    unnamed x1, local copies, waits for them, and re-layouts  0.75 us

profile of v3, /device:TPU:6, one launch (start us, length us, event | category | flops | bytes accessed | tf_op | source)
XLA Modules:
  0.0 31.7 jit_solution(12987174283817078796)
XLA Ops:
  0.0 30.9 %shard_map.28 = f32[3,32,8,128]{3,2,1,0:T(8,128)S(1)} custom-call(f32[3,32,8,128]{3,2,1,0:T(8,128)} %bitcast.4, f32[32,8,128]{2,1,0:T(8,128)} %bitcast.5), custom_call_target="tpu_custom_call" | custom-call | tf_op jit(solution)/shard_map/pallas_call | solution.py:268
  30.9 0.7 %copy.4 = f32[1,3,16,16,128]{4,3,2,1,0:T(8,128)} copy(f32[1,3,16,16,128]{4,3,2,1,0:T(8,128)S(1)} %bitcast.3) | data formatting | bytes 786432

commit v4 on v3

--- a/solution.py
+++ b/solution.py
@@ -13,6 +13,7 @@
 ROWS = 8
 SLABS = 4
 WIDE = 3 * STEPS
+NEXT = 4
 OWN = 16
 SPAN = OWN + 2 * WIDE
 GROUPS = 4
@@ -52,9 +53,9 @@
 def kernel(states, rate_in, out, rate, w0, w1, w2, w3, w4, w5, jump, got, total, tots, path,
            load_sem, halo_send, halo_recv, up_send, up_recv, row_send, row_recv, down_send, down_recv, own_sem):
     tm, gz = lax.axis_index("tm"), lax.axis_index("gz")
-    zi, row = lax.rem(tm, RING), lax.div(tm, RING)
-    above, below = lax.rem(gz + 1, SLABS), lax.rem(gz + SLABS - 1, SLABS)
-    far = lax.rem(gz, 2)
+    zi, row = tm & (RING - 1), tm // RING
+    above, below = (gz + 1) & (SLABS - 1), (gz + SLABS - 1) & (SLABS - 1)
+    far = gz & 1
     start = row * RING
 
     load = pltpu.make_async_copy(states, w0.at[:, pl.ds(2 * WIDE, 2 * OWN)], load_sem.at[0])
@@ -65,23 +66,23 @@
     for peer in (above, below):
         pl.semaphore_signal(barrier, inc=1, device_id={"gz": peer}, device_id_type=MESH)
     for q in range(1, RING):
-        pl.semaphore_signal(barrier, inc=1, device_id={"tm": start + lax.rem(zi + q, RING)}, device_id_type=MESH)
+        pl.semaphore_signal(barrier, inc=1, device_id={"tm": start + ((zi + q) & (RING - 1))}, device_id_type=MESH)
 
     def greet(q, carry):
         pl.semaphore_signal(barrier, inc=1, device_id={"tm": q * RING + zi}, device_id_type=MESH)
         return carry
 
     lax.fori_loop(0, row, greet, 0)
-    pl.semaphore_wait(barrier, 2 + (RING - 1) + (ROWS - 1 - row))
-
-    down_halo = pltpu.make_async_remote_copy(
-        states.at[:, pl.ds(0, 2 * WIDE)], w0.at[:, pl.ds(2 * (OWN + WIDE), 2 * WIDE)], halo_send.at[0], halo_recv.at[1],
-        device_id={"gz": below}, device_id_type=MESH)
-    up_halo = pltpu.make_async_remote_copy(
-        states.at[:, pl.ds(2 * (OWN - WIDE), 2 * WIDE)], w0.at[:, pl.ds(0, 2 * WIDE)], halo_send.at[1], halo_recv.at[0],
-        device_id={"gz": above}, device_id_type=MESH)
-    down_halo.start()
-    up_halo.start()
+    def halo(upper, outer):
+        planes = WIDE - NEXT if outer else NEXT
+        if upper:
+            source, target = (NEXT if outer else 0), OWN + WIDE + (NEXT if outer else 0)
+        else:
+            source, target = OWN - (WIDE if outer else NEXT), (0 if outer else WIDE - NEXT)
+        return pltpu.make_async_remote_copy(
+            w0.at[:, pl.ds(2 * (WIDE + source), 2 * planes)], w0.at[:, pl.ds(2 * target, 2 * planes)],
+            halo_send.at[upper, outer], halo_recv.at[upper, outer],
+            device_id={"gz": below if upper else above}, device_id_type=MESH)
 
     @pl.when(tm == 0)
     def _():
@@ -90,8 +91,8 @@
     works = (w0, w1, w2, w3, w4, w5)
     keep_own = jnp.where(tm == 0, 0.0, 1.0)
 
-    def stages(first_plane, count, at_once):
-        for k in range(1, 2 * 3 + 1):
+    def stages(first_plane, count, at_once, ks=range(1, 7)):
+        for k in ks:
             src, base = works[k - 1], works[3 * ((k - 1) // 3)]
             kind = (k - 1) % 3
             begin = first_plane(k)
@@ -128,7 +129,7 @@
 
     def send_up(group):
         for q in (4, 3, 5, 2, 6, 1, 7):
-            peer = lax.rem(zi + q, RING)
+            peer = ((zi + q) & (RING - 1))
             pltpu.make_async_remote_copy(
                 jump.at[:, tile_of(group, peer)], got.at[group, zi], up_send.at[group], up_recv.at[group],
                 device_id={"tm": start + peer}, device_id_type=MESH).start()
@@ -181,7 +182,7 @@
                 acc = [damp * acc[c] + got[group, z, c] for c in range(3)]
         mine = tile_of(group, zi)
         for q in (4, 3, 5, 2, 6, 1, 7):
-            peer = lax.rem(zi + q, RING)
+            peer = ((zi + q) & (RING - 1))
 
             @pl.when(start + peer > 0)
             def _():
@@ -195,24 +196,41 @@
 
     load.wait()
     load_rate.wait()
-    stages(lambda k: WIDE + k, lambda k: OWN - 2 * k, (7, 6, 5, 8, 6, 4))
+    inside = lambda ks: stages(lambda k: WIDE + k, lambda k: OWN - 2 * k, (7, 6, 5, 8, 6, 4), ks)
+    inside(range(1, 5))
+    pl.semaphore_wait(barrier, 2 + (RING - 1) + (ROWS - 1 - row))
+
+
+    for upper in (0, 1):
+        @pl.when(upper == 1 - far)
+        def _(upper=upper):
+            halo(1 - upper, 0).start()
+            halo(upper, 0).start()
+            halo(upper, 1).start()
+            halo(1 - upper, 1).start()
+
+    inside(range(5, 7))
     send_up(0)
 
-    def side(upper):
-        @pl.when(upper == 0)
-        def _():
-            up_halo.wait_recv()
-
-        @pl.when(upper == 1)
-        def _():
-            down_halo.wait_recv()
-
-        stages(lambda k: jnp.where(upper == 1, OWN + WIDE - k, k), lambda k: WIDE, (6,) * 6)
-
-    side(1 - far)
+    def halo_wait(upper, outers):
+        for choice in (0, 1):
+            @pl.when(upper == choice)
+            def _(choice=choice):
+                for outer in outers:
+                    halo(choice, outer).wait_recv()
+
+    def side(upper, skip, planes):
+        stages(lambda k: jnp.where(upper == 1, SPAN - WIDE + skip - k, WIDE - skip - planes + k), lambda k: planes, (planes,) * 6)
+
+    near_upper, far_upper = 1 - far, far
+    halo_wait(near_upper, (0, 1))
+    side(near_upper, 0, WIDE)
     send_up(1)
-    side(far)
+    halo_wait(far_upper, (0,))
+    side(far_upper, 0, NEXT)
     send_up(2)
+    halo_wait(far_upper, (1,))
+    side(far_upper, NEXT, WIDE - NEXT)
     send_up(3)
     sum_row(0)
     sum_row(1)
@@ -235,7 +253,7 @@
 
         lax.fori_loop(row + 1, ROWS, told, 0)
         for q in range(1, RING):
-            peer, source = lax.rem(zi + q, RING), lax.rem(zi + RING - q, RING)
+            peer, source = ((zi + q) & (RING - 1)), ((zi + RING - q) & (RING - 1))
 
             @pl.when(start + peer > 0)
             def _():
@@ -257,8 +275,9 @@
     def _():
         pltpu.make_async_copy(states, out, own_sem.at[0]).wait()
 
-    down_halo.wait_send()
-    up_halo.wait_send()
+    for upper in (0, 1):
+        for outer in (0, 1):
+            halo(upper, outer).wait_send()
 
 
 def shards(states, rate):
@@ -276,7 +295,7 @@
             pltpu.VMEM((GROUPS, 3, 8, 128), f32),
             pltpu.VMEM((GROUPS, ROWS, 3, 8, 128), f32),
             pltpu.VMEM((GROUPS, RING, 3, 8, 128), f32),
-            dma((2,)), dma((2,)), dma((2,)), dma((GROUPS,)), dma((GROUPS,)),
+            dma((2,)), dma((2, 2)), dma((2, 2)), dma((GROUPS,)), dma((GROUPS,)),
             dma((GROUPS, ROWS)), dma((GROUPS, ROWS)), dma((GROUPS, RING)), dma((GROUPS, RING)), dma((GROUPS,)),
         ],
         compiler_params=pltpu.CompilerParams(collective_id=0, has_side_effects=True, vmem_limit_bytes=32 * 1024 * 1024),

time: 32.3 us -> 31.6 us (0.978)
  the two profiles are of different devices: /device:TPU:6 before, /device:TPU:15 now
where the time goes in v4:
time: 31.6 us; the launch traced here: 31.5 us
  Pallas kernels  30.7 us (97%)
  local copies, waits for them, and re-layouts  0.75 us (2%)
    pallas_call x1, Pallas kernels, shards(): pl.pallas_call(kernel, out_shape=jax.ShapeDtypeStruct((3, 2 * OWN, 8, 128...  30.7 us
    unnamed x1, local copies, waits for them, and re-layouts  0.75 us

profile of v4, /device:TPU:15, one launch (start us, length us, event | category | flops | bytes accessed | tf_op | source)
XLA Modules:
  0.0 31.5 jit_solution(10419252364402925720)
XLA Ops:
  0.0 30.7 %shard_map.28 = f32[3,32,8,128]{3,2,1,0:T(8,128)S(1)} custom-call(f32[3,32,8,128]{3,2,1,0:T(8,128)} %bitcast.4, f32[32,8,128]{2,1,0:T(8,128)} %bitcast.5), custom_call_target="tpu_custom_call" | custom-call | tf_op jit(solution)/shard_map/pallas_call | solution.py:287
  30.7 0.7 %copy.4 = f32[1,3,16,16,128]{4,3,2,1,0:T(8,128)} copy(f32[1,3,16,16,128]{4,3,2,1,0:T(8,128)S(1)} %bitcast.3) | data formatting | bytes 786432

commit v5 on v4

--- a/solution.py
+++ b/solution.py
@@ -160,7 +160,7 @@
                 device_id={"tm": later * RING + zi}, device_id_type=MESH).start()
             return carry
 
-        lax.fori_loop(row + 1, ROWS, tell, 0)
+        lax.fori_loop(0, ROWS - 1 - row, lambda i, carry: tell(ROWS - 1 - i, carry), 0)
 
     def send_down(group):
         damp = damp_of(group)
@@ -229,10 +229,10 @@
     halo_wait(far_upper, (0,))
     side(far_upper, 0, NEXT)
     send_up(2)
+    sum_row(0)
     halo_wait(far_upper, (1,))
     side(far_upper, NEXT, WIDE - NEXT)
     send_up(3)
-    sum_row(0)
     sum_row(1)
     send_down(0)
     sum_row(2)

time: 31.6 us -> 30.9 us (0.978)
  the two profiles are of different devices: /device:TPU:15 before, /device:TPU:6 now
where the time goes in v5:
time: 30.9 us; the launch traced here: 30.4 us
  Pallas kernels  29.7 us (96%)
  local copies, waits for them, and re-layouts  0.75 us (2%)
    pallas_call x1, Pallas kernels, shards(): pl.pallas_call(kernel, out_shape=jax.ShapeDtypeStruct((3, 2 * OWN, 8, 128...  29.7 us
    unnamed x1, local copies, waits for them, and re-layouts  0.75 us

profile of v5, /device:TPU:6, one launch (start us, length us, event | category | flops | bytes accessed | tf_op | source)
XLA Modules:
  0.0 30.4 jit_solution(16359205061698686994)
XLA Ops:
  0.0 29.7 %shard_map.28 = f32[3,32,8,128]{3,2,1,0:T(8,128)S(1)} custom-call(f32[3,32,8,128]{3,2,1,0:T(8,128)} %bitcast.4, f32[32,8,128]{2,1,0:T(8,128)} %bitcast.5), custom_call_target="tpu_custom_call" | custom-call | tf_op jit(solution)/shard_map/pallas_call | solution.py:287
  29.7 0.7 %copy.4 = f32[1,3,16,16,128]{4,3,2,1,0:T(8,128)} copy(f32[1,3,16,16,128]{4,3,2,1,0:T(8,128)S(1)} %bitcast.3) | data formatting | bytes 786432

commit v6 on v5

--- a/solution.py
+++ b/solution.py
@@ -13,7 +13,7 @@
 ROWS = 8
 SLABS = 4
 WIDE = 3 * STEPS
-NEXT = 4
+NEXT = 2
 OWN = 16
 SPAN = OWN + 2 * WIDE
 GROUPS = 4
@@ -120,12 +120,10 @@
             else:
                 lax.fori_loop(0, turns, turn, 0)
 
-    bases = (6, 10 - 8 * far, 2 + 8 * far)
-
     def tile_of(group, k):
-        if group < 3:
-            return 2 * bases[group] + k
-        return k + jnp.where(k >= 4, 24, 0)
+        if group == 2:
+            return k + jnp.where(k >= 4, 4 + 12 * far, 28 - 28 * far)
+        return k + (12, 20 - 16 * far, None, 24 * far)[group]
 
     def send_up(group):
         for q in (4, 3, 5, 2, 6, 1, 7):
@@ -197,9 +195,8 @@
     load.wait()
     load_rate.wait()
     inside = lambda ks: stages(lambda k: WIDE + k, lambda k: OWN - 2 * k, (7, 6, 5, 8, 6, 4), ks)
-    inside(range(1, 5))
+    inside(range(1, 3))
     pl.semaphore_wait(barrier, 2 + (RING - 1) + (ROWS - 1 - row))
-
 
     for upper in (0, 1):
         @pl.when(upper == 1 - far)
@@ -209,7 +206,7 @@
             halo(upper, 1).start()
             halo(1 - upper, 1).start()
 
-    inside(range(5, 7))
+    inside(range(3, 7))
     send_up(0)
 
     def halo_wait(upper, outers):

time: 30.9 us -> 30.2 us (0.977)
  Pallas kernels: 29.7 us -> 29.2 us
    pallas_call x1, Pallas kernels: 29.7 us -> 29.2 us  [shards(): pl.pallas_call(kernel, out_shape=jax.ShapeDtypeStruct((3, 2 * OWN, 8, 128...]
where the time goes in v6:
time: 30.2 us; the launch traced here: 30 us
  Pallas kernels  29.2 us (97%)
  local copies, waits for them, and re-layouts  0.75 us (2%)
    pallas_call x1, Pallas kernels, shards(): pl.pallas_call(kernel, out_shape=jax.ShapeDtypeStruct((3, 2 * OWN, 8, 128...  29.2 us
    unnamed x1, local copies, waits for them, and re-layouts  0.75 us

profile of v6, /device:TPU:6, one launch (start us, length us, event | category | flops | bytes accessed | tf_op | source)
XLA Modules:
  0.0 30.0 jit_solution(8961078055165942834)
XLA Ops:
  0.0 29.2 %shard_map.28 = f32[3,32,8,128]{3,2,1,0:T(8,128)S(1)} custom-call(f32[3,32,8,128]{3,2,1,0:T(8,128)} %bitcast.4, f32[32,8,128]{2,1,0:T(8,128)} %bitcast.5), custom_call_target="tpu_custom_call" | custom-call | tf_op jit(solution)/shard_map/pallas_call | solution.py:284
  29.2 0.7 %copy.4 = f32[1,3,16,16,128]{4,3,2,1,0:T(8,128)} copy(f32[1,3,16,16,128]{4,3,2,1,0:T(8,128)S(1)} %bitcast.3) | data formatting | bytes 786432

commit v7 on v6

--- a/solution.py
+++ b/solution.py
@@ -90,6 +90,7 @@
 
     works = (w0, w1, w2, w3, w4, w5)
     keep_own = jnp.where(tm == 0, 0.0, 1.0)
+    busy = tm < SLICES - 1
 
     def stages(first_plane, count, at_once, ks=range(1, 7)):
         for k in ks:
@@ -132,25 +133,39 @@
                 jump.at[:, tile_of(group, peer)], got.at[group, zi], up_send.at[group], up_recv.at[group],
                 device_id={"tm": start + peer}, device_id_type=MESH).start()
 
-    def all_of(buf, send, recv):
+    def all_of(buf, send, recv, count=RING - 1):
         return pltpu.make_async_remote_copy(
-            buf.at[pl.ds(0, RING - 1)], buf.at[pl.ds(0, RING - 1)], send, recv,
+            buf.at[pl.ds(0, count)], buf.at[pl.ds(0, count)], send, recv,
             device_id={"tm": tm}, device_id_type=MESH)
 
     def damp_of(group):
         return jnp.exp(rate[tile_of(group, zi)] * (-1.0 / SLICES))
 
     def sum_row(group):
-        all_of(got.at[group], up_send.at[group], up_recv.at[group]).wait_recv()
-        mine = tile_of(group, zi)
-        for c in range(3):
-            got[group, zi, c] = jump[c, mine]
-        damp = damp_of(group)
-        acc = [got[group, 0, c] for c in range(3)]
-        for z in range(1, RING):
-            acc = [damp * acc[c] + got[group, z, c] for c in range(3)]
-        for c in range(3):
-            total[group, c] = acc[c]
+        short = (row == ROWS - 1) & (zi < RING - 1)
+
+        @pl.when(short)
+        def _():
+            all_of(got.at[group], up_send.at[group], up_recv.at[group], RING - 2).wait_recv()
+
+        @pl.when(jnp.logical_not(short))
+        def _():
+            all_of(got.at[group], up_send.at[group], up_recv.at[group]).wait_recv()
+
+        @pl.when(busy)
+        def _():
+            mine = tile_of(group, zi)
+            for c in range(3):
+                got[group, zi, c] = jump[c, mine]
+
+        @pl.when(row < ROWS - 1)
+        def _():
+            damp = damp_of(group)
+            acc = [got[group, 0, c] for c in range(3)]
+            for z in range(1, RING):
+                acc = [damp * acc[c] + got[group, z, c] for c in range(3)]
+            for c in range(3):
+                total[group, c] = acc[c]
 
         def tell(later, carry):
             pltpu.make_async_remote_copy(
@@ -192,23 +207,6 @@
         def _():
             pltpu.make_async_copy(path.at[group, zi], out.at[:, mine], own_sem.at[group]).start()
 
-    load.wait()
-    load_rate.wait()
-    inside = lambda ks: stages(lambda k: WIDE + k, lambda k: OWN - 2 * k, (7, 6, 5, 8, 6, 4), ks)
-    inside(range(1, 3))
-    pl.semaphore_wait(barrier, 2 + (RING - 1) + (ROWS - 1 - row))
-
-    for upper in (0, 1):
-        @pl.when(upper == 1 - far)
-        def _(upper=upper):
-            halo(1 - upper, 0).start()
-            halo(upper, 0).start()
-            halo(upper, 1).start()
-            halo(1 - upper, 1).start()
-
-    inside(range(3, 7))
-    send_up(0)
-
     def halo_wait(upper, outers):
         for choice in (0, 1):
             @pl.when(upper == choice)
@@ -219,17 +217,44 @@
     def side(upper, skip, planes):
         stages(lambda k: jnp.where(upper == 1, SPAN - WIDE + skip - k, WIDE - skip - planes + k), lambda k: planes, (planes,) * 6)
 
+    load.wait()
+    load_rate.wait()
+    inside = lambda ks: stages(lambda k: WIDE + k, lambda k: OWN - 2 * k, (7, 6, 5, 8, 6, 4), ks)
     near_upper, far_upper = 1 - far, far
-    halo_wait(near_upper, (0, 1))
-    side(near_upper, 0, WIDE)
-    send_up(1)
-    halo_wait(far_upper, (0,))
-    side(far_upper, 0, NEXT)
-    send_up(2)
+
+    @pl.when(busy)
+    def _():
+        inside(range(1, 3))
+
+    pl.semaphore_wait(barrier, 2 + (RING - 1) + (ROWS - 1 - row))
+
+    @pl.when(busy)
+    def _():
+        for upper in (0, 1):
+            @pl.when(upper == 1 - far)
+            def _(upper=upper):
+                halo(1 - upper, 0).start()
+                halo(upper, 0).start()
+                halo(upper, 1).start()
+                halo(1 - upper, 1).start()
+
+        inside(range(3, 7))
+        send_up(0)
+        halo_wait(near_upper, (0, 1))
+        side(near_upper, 0, WIDE)
+        send_up(1)
+        halo_wait(far_upper, (0,))
+        side(far_upper, 0, NEXT)
+        send_up(2)
+
     sum_row(0)
-    halo_wait(far_upper, (1,))
-    side(far_upper, NEXT, WIDE - NEXT)
-    send_up(3)
+
+    @pl.when(busy)
+    def _():
+        halo_wait(far_upper, (1,))
+        side(far_upper, NEXT, WIDE - NEXT)
+        send_up(3)
+
     sum_row(1)
     send_down(0)
     sum_row(2)
@@ -240,7 +265,10 @@
 
     for group in range(GROUPS):
         mine = tile_of(group, zi)
-        all_of(got.at[group], up_send.at[group], up_recv.at[group]).wait_send()
+        @pl.when(busy)
+        def _(group=group):
+            all_of(got.at[group], up_send.at[group], up_recv.at[group]).wait_send()
+
 
         def told(later, carry, group=group):
             pltpu.make_async_remote_copy(
@@ -272,9 +300,11 @@
     def _():
         pltpu.make_async_copy(states, out, own_sem.at[0]).wait()
 
-    for upper in (0, 1):
-        for outer in (0, 1):
-            halo(upper, outer).wait_send()
+    @pl.when(busy)
+    def _():
+        for upper in (0, 1):
+            for outer in (0, 1):
+                halo(upper, outer).wait_send()
 
 
 def shards(states, rate):

time: 30.2 us -> 30.2 us (level)
  no operation moved by 1% of the time
where the time goes in v7:
time: 30.2 us; the launch traced here: 30 us
  Pallas kernels  29.2 us (97%)
  local copies, waits for them, and re-layouts  0.75 us (2%)
    pallas_call x1, Pallas kernels, shards(): pl.pallas_call(kernel, out_shape=jax.ShapeDtypeStruct((3, 2 * OWN, 8, 128...  29.2 us
    unnamed x1, local copies, waits for them, and re-layouts  0.75 us

profile of v7, /device:TPU:6, one launch (start us, length us, event | category | flops | bytes accessed | tf_op | source)
XLA Modules:
  0.0 30.0 jit_solution(11655766177505786579)
XLA Ops:
  0.0 29.2 %shard_map.28 = f32[3,32,8,128]{3,2,1,0:T(8,128)S(1)} custom-call(f32[3,32,8,128]{3,2,1,0:T(8,128)} %bitcast.4, f32[32,8,128]{2,1,0:T(8,128)} %bitcast.5), custom_call_target="tpu_custom_call" | custom-call | tf_op jit(solution)/shard_map/pallas_call | solution.py:314
  29.2 0.7 %copy.4 = f32[1,3,16,16,128]{4,3,2,1,0:T(8,128)} copy(f32[1,3,16,16,128]{4,3,2,1,0:T(8,128)S(1)} %bitcast.3) | data formatting | bytes 786432

commit v8 on v7

--- a/solution.py
+++ b/solution.py
@@ -167,13 +167,12 @@
             for c in range(3):
                 total[group, c] = acc[c]
 
-        def tell(later, carry):
-            pltpu.make_async_remote_copy(
-                total.at[group], tots.at[group, row], row_send.at[group, later], row_recv.at[group, row],
-                device_id={"tm": later * RING + zi}, device_id_type=MESH).start()
-            return carry
-
-        lax.fori_loop(0, ROWS - 1 - row, lambda i, carry: tell(ROWS - 1 - i, carry), 0)
+        for ahead in range(ROWS - 1, 0, -1):
+            @pl.when(row + ahead < ROWS)
+            def _(ahead=ahead):
+                pltpu.make_async_remote_copy(
+                    total.at[group], tots.at[group, row], row_send.at[group, ahead], row_recv.at[group, row],
+                    device_id={"tm": (row + ahead) * RING + zi}, device_id_type=MESH).start()
 
     def send_down(group):
         damp = damp_of(group)
@@ -194,7 +193,7 @@
             if z < RING - 1:
                 acc = [damp * acc[c] + got[group, z, c] for c in range(3)]
         mine = tile_of(group, zi)
-        for q in (4, 3, 5, 2, 6, 1, 7):
+        for q in (4, 5, 3, 6, 2, 7, 1):
             peer = ((zi + q) & (RING - 1))
 
             @pl.when(start + peer > 0)
@@ -218,7 +217,6 @@
         stages(lambda k: jnp.where(upper == 1, SPAN - WIDE + skip - k, WIDE - skip - planes + k), lambda k: planes, (planes,) * 6)
 
     load.wait()
-    load_rate.wait()
     inside = lambda ks: stages(lambda k: WIDE + k, lambda k: OWN - 2 * k, (7, 6, 5, 8, 6, 4), ks)
     near_upper, far_upper = 1 - far, far
 
@@ -227,6 +225,7 @@
         inside(range(1, 3))
 
     pl.semaphore_wait(barrier, 2 + (RING - 1) + (ROWS - 1 - row))
+    load_rate.wait()
 
     @pl.when(busy)
     def _():
@@ -270,13 +269,13 @@
             all_of(got.at[group], up_send.at[group], up_recv.at[group]).wait_send()
 
 
-        def told(later, carry, group=group):
-            pltpu.make_async_remote_copy(
-                total.at[group], tots.at[group, row], row_send.at[group, later], row_recv.at[group, row],
-                device_id={"tm": later * RING + zi}, device_id_type=MESH).wait_send()
-            return carry
-
-        lax.fori_loop(row + 1, ROWS, told, 0)
+        for ahead in range(1, ROWS):
+            @pl.when(row + ahead < ROWS)
+            def _(ahead=ahead, group=group):
+                pltpu.make_async_remote_copy(
+                    total.at[group], tots.at[group, row], row_send.at[group, ahead], row_recv.at[group, row],
+                    device_id={"tm": (row + ahead) * RING + zi}, device_id_type=MESH).wait_send()
+
         for q in range(1, RING):
             peer, source = ((zi + q) & (RING - 1)), ((zi + RING - q) & (RING - 1))
 

time: 30.2 us -> 30.2 us (level)
  no operation moved by 1% of the time
where the time goes in v8:
time: 30.2 us; the launch traced here: 30.1 us
  Pallas kernels  29.3 us (97%)
  local copies, waits for them, and re-layouts  0.75 us (2%)
    pallas_call x1, Pallas kernels, shards(): pl.pallas_call(kernel, out_shape=jax.ShapeDtypeStruct((3, 2 * OWN, 8, 128...  29.3 us
    unnamed x1, local copies, waits for them, and re-layouts  0.75 us

profile of v8, /device:TPU:6, one launch (start us, length us, event | category | flops | bytes accessed | tf_op | source)
XLA Modules:
  0.0 30.1 jit_solution(8793596391274860819)
XLA Ops:
  0.0 29.3 %shard_map.28 = f32[3,32,8,128]{3,2,1,0:T(8,128)S(1)} custom-call(f32[3,32,8,128]{3,2,1,0:T(8,128)} %bitcast.4, f32[32,8,128]{2,1,0:T(8,128)} %bitcast.5), custom_call_target="tpu_custom_call" | custom-call | tf_op jit(solution)/shard_map/pallas_call | solution.py:313
  29.3 0.7 %copy.4 = f32[1,3,16,16,128]{4,3,2,1,0:T(8,128)} copy(f32[1,3,16,16,128]{4,3,2,1,0:T(8,128)S(1)} %bitcast.3) | data formatting | bytes 786432
